TPU v7x, 32 devices: a whole 2x2x4 slice. The times are simulated.
32 devices in a mesh: blk: 8 (over z, y), quarter: 4 (over x, core).
Axes of the slice: x: 2, y: 2, z: 4, core: 2. Of those that a mesh axis runs over, the one named last changes fastest.
Arguments:
- start: float32 [2048, 2, 2048], P(('blk', 'quarter')), may hold values from -6 to 6
- observed: float32 [4, 16, 4096], P(None, 'blk', 'quarter'), may hold values from -6 to 6
- coverage: int32 [4, 16, 4096], P(None, 'blk', 'quarter'), may hold values from 0 to 4
- class_weight: float32 [4, 4], replicated, may hold values from 0.25 to 4
- degree_gain: float32 [4, 2048], replicated, may hold values from 0.5 to 2
- legendre: bfloat16 [2048, 8, 2048], P(('blk', 'quarter')), as said below
- order_table: int32 [2048], replicated, may hold values from 0 to 2047, as said below
Outputs:
- solution: float32 [2048, 2, 2048], P(('blk', 'quarter'))
- gradient: float32 [2048, 2, 2048], P(('blk', 'quarter'))
Inputs may be any that keep to these rules, and one draw needn't show every extreme that they name: `order_table`: slots 2i and 2i + 1 hold the orders i and 2047 - i, one each, for every i below 1024. legendre[s, j, l] is zero wherever the degree l is below the order of slot s.
All inputs are finite; a program needn't handle non-finite values.
Results may differ from a plain program's by a relative error of at most 0.02.
Values may be sent and summed in bfloat16 or wider, within the bound.
A program may use at most 128 MiB of HBM per device.

v0:
```python
import functools
import math

import jax
import jax.numpy as jnp
from jax import lax
from jax.experimental import pallas as pl
from jax.experimental.pallas import tpu as pltpu
from jax.sharding import PartitionSpec as P

ITERS = 2
MESH = pl.DeviceIdType.MESH


def exchange_kernel(blk_count, quarter_count, per_blk, send_ref, recv_ref, send_sem, recv_sem):
    total = blk_count * quarter_count
    blk = lax.axis_index("blk")
    quarter = lax.axis_index("quarter")
    me = blk * quarter_count + quarter
    barrier = pltpu.get_barrier_semaphore()

    def greet(i, carry):
        peer = lax.rem(me + i, total)
        pl.semaphore_signal(
            barrier,
            inc=1,
            device_id=(lax.div(peer, quarter_count), lax.rem(peer, quarter_count)),
            device_id_type=MESH,
        )
        return carry

    lax.fori_loop(1, total, greet, 0)
    recv_ref[me] = send_ref[blk if per_blk else me]
    pl.semaphore_wait(barrier, total - 1)

    def send(i, carry):
        peer = lax.rem(me + i, total)
        peer_blk = lax.div(peer, quarter_count)
        pltpu.make_async_remote_copy(
            src_ref=send_ref.at[peer_blk if per_blk else peer],
            dst_ref=recv_ref.at[me],
            send_sem=send_sem,
            recv_sem=recv_sem,
            device_id=(peer_blk, lax.rem(peer, quarter_count)),
            device_id_type=MESH,
        ).start()
        return carry

    lax.fori_loop(1, total, send, 0)
    landed = recv_ref.at[pl.ds(0, total - 1)]
    pltpu.make_async_copy(landed, landed, recv_sem).wait()
    pltpu.make_async_copy(landed, landed, send_sem).wait()


def exchange(messages, blk_count, quarter_count, per_blk):
    total = blk_count * quarter_count
    return pl.pallas_call(
        functools.partial(exchange_kernel, blk_count, quarter_count, per_blk),
        out_shape=jax.ShapeDtypeStruct((total,) + messages.shape[1:], messages.dtype),
        in_specs=[pl.BlockSpec(memory_space=pltpu.VMEM)],
        out_specs=pl.BlockSpec(memory_space=pltpu.VMEM),
        scratch_shapes=[pltpu.SemaphoreType.DMA(()), pltpu.SemaphoreType.DMA(())],
        compiler_params=pltpu.CompilerParams(
            collective_id=0 if per_blk else 1, has_side_effects=True, vmem_limit_bytes=32 << 20
        ),
        name="to_cycles" if per_blk else "to_orders",
    )(messages)


def scatter(me, blk_count, quarter_count, send_ref, per_blk, recv_ref, send_sem, recv_sem):
    total = blk_count * quarter_count

    def send(i, carry):
        peer = lax.rem(me + i, total)
        peer_blk = lax.div(peer, quarter_count)
        pltpu.make_async_remote_copy(
            src_ref=send_ref.at[peer_blk if per_blk else peer],
            dst_ref=recv_ref.at[me],
            send_sem=send_sem,
            recv_sem=recv_sem,
            device_id=(peer_blk, lax.rem(peer, quarter_count)),
            device_id_type=MESH,
        ).start()
        return carry

    lax.fori_loop(1, total, send, 0)


def grid_kernel(
    blk_count,
    quarter_count,
    scale,
    params_ref,
    send_ref,
    old_ref,
    weight_ref,
    cos_ref,
    sin_ref,
    table_ref,
    returned_ref,
    image_ref,
    sums_ref,
    arrived_ref,
    left_ref,
    shares_ref,
    landed_ref,
    send_sem,
    recv_sem,
):
    total = blk_count * quarter_count
    blk = lax.axis_index("blk")
    quarter = lax.axis_index("quarter")
    me = blk * quarter_count + quarter
    barrier = pltpu.get_barrier_semaphore()

    def greet(i, carry):
        peer = lax.rem(me + i, total)
        pl.semaphore_signal(
            barrier,
            inc=1,
            device_id=(lax.div(peer, quarter_count), lax.rem(peer, quarter_count)),
            device_id_type=MESH,
        )
        return carry

    lax.fori_loop(1, total, greet, 0)
    arrived_ref[me] = send_ref[blk]
    pl.semaphore_wait(barrier, total - 1)
    scatter(me, blk_count, quarter_count, send_ref, True, arrived_ref, send_sem.at[0], recv_sem.at[0])
    some = arrived_ref.at[pl.ds(0, total - 1)]
    pltpu.make_async_copy(some, some, recv_sem.at[0]).wait()

    arrived = arrived_ref[...].astype(jnp.float32)
    rows = arrived.shape[1] // 2
    lanes = arrived.shape[2]
    lane = lax.broadcasted_iota(jnp.int32, (1, 1, lanes), 2)
    sign = jnp.where(lane < lanes // 2, jnp.float32(1.0), jnp.float32(-1.0))
    values = arrived[:, :rows]
    turned = values * cos_ref[...] + pltpu.roll(values, lanes // 2, 2) * sin_ref[...]
    left = jnp.concatenate([turned, turned * sign], 1).astype(jnp.bfloat16)
    for d in range(total):
        left_ref[:, d * lanes : (d + 1) * lanes] = left[d]
    tail = jnp.sum(arrived[:, rows:], 0)
    energy = jnp.sum(jnp.sum(tail, 1, keepdims=True), 0, keepdims=True)

    field = scale * jnp.dot(left_ref[...], table_ref[...], preferred_element_type=jnp.float32)
    params = params_ref[...]
    ratio = params[1:2, 0:1] + params[2:3, 0:1] * energy / params[3:4, 0:1]
    image = params[0:1, 0:1] * field + ratio * old_ref[...]
    image_ref[...] = image
    weighted = weight_ref[...] * image
    partial = jnp.sum(weighted * image, 0, keepdims=True)
    partial = sum(partial[:, i : i + lanes] for i in range(0, partial.shape[1], lanes))
    high = partial.astype(jnp.bfloat16).astype(jnp.float32)
    middle = (partial - high).astype(jnp.bfloat16).astype(jnp.float32)
    low = partial - high - middle
    row = lax.broadcasted_iota(jnp.int32, (rows, lanes), 0)
    tail = jnp.where(row == 0, high, jnp.where(row == 1, middle, jnp.where(row == 2, low, 0.0)))
    plus, minus = weighted[:rows], weighted[rows:]
    folded = jnp.concatenate([plus + minus, plus - minus], 0).astype(jnp.bfloat16)
    back = lax.dot_general(
        folded, table_ref[...], (((1,), (1,)), ((), ())), preferred_element_type=jnp.float32
    )
    cos_lanes = lax.broadcasted_iota(jnp.int32, (rows, lanes), 1) < lanes // 2
    for d in range(total):
        part = back[:, d * lanes : (d + 1) * lanes]
        picked = scale * jnp.where(cos_lanes, part[:rows], part[rows:])
        share = picked * cos_ref[d] - pltpu.roll(picked, lanes // 2, 1) * sin_ref[d]
        shares_ref[d] = jnp.concatenate([share, tail], 0).astype(jnp.bfloat16)

    landed_ref[me] = shares_ref[me]
    scatter(me, blk_count, quarter_count, shares_ref, False, landed_ref, send_sem.at[1], recv_sem.at[1])
    some = landed_ref.at[pl.ds(0, total - 1)]
    pltpu.make_async_copy(some, some, recv_sem.at[1]).wait()
    landed = landed_ref[...].astype(jnp.float32)
    for b in range(blk_count):
        returned_ref[b] = sum(landed[b * quarter_count + q, :rows] for q in range(quarter_count))
    tail = jnp.sum(landed[:, rows:], 0)
    curvature = jnp.sum(jnp.sum(tail, 1, keepdims=True), 0, keepdims=True)
    sums_ref[...] = jnp.where(row == 0, energy, curvature)
    pltpu.make_async_copy(some, some, send_sem.at[0]).wait()
    pltpu.make_async_copy(some, some, send_sem.at[1]).wait()


def grid_stage(params, messages, old, weight, cos_rot, sin_rot, table, blk_count, quarter_count, scale):
    total = blk_count * quarter_count
    block_rows, lanes = messages.shape[1:]
    rows = block_rows // 2
    block = (total, block_rows, lanes)
    return pl.pallas_call(
        functools.partial(grid_kernel, blk_count, quarter_count, scale),
        out_shape=(
            jax.ShapeDtypeStruct((blk_count, rows, lanes), jnp.float32),
            jax.ShapeDtypeStruct(old.shape, jnp.float32),
            jax.ShapeDtypeStruct((rows, lanes), jnp.float32),
        ),
        in_specs=[pl.BlockSpec(memory_space=pltpu.VMEM)] * 7,
        out_specs=(pl.BlockSpec(memory_space=pltpu.VMEM),) * 3,
        scratch_shapes=[
            pltpu.VMEM(block, jnp.bfloat16),
            pltpu.VMEM((block_rows, total * lanes), jnp.bfloat16),
            pltpu.VMEM(block, jnp.bfloat16),
            pltpu.VMEM(block, jnp.bfloat16),
            pltpu.SemaphoreType.DMA((2,)),
            pltpu.SemaphoreType.DMA((2,)),
        ],
        compiler_params=pltpu.CompilerParams(
            collective_id=2, has_side_effects=True, vmem_limit_bytes=24 << 20
        ),
        name="grid_stage",
    )(params, messages, old, weight, cos_rot, sin_rot, table)


def half_turn_sine(phase, quarter_turn):
    z = phase.astype(jnp.float32) * (1.0 / quarter_turn)
    y = z * z
    acc = jnp.float32(-3.41817280e-06)
    for coef in (1.60217136e-04, -4.68162024e-03, 7.96925873e-02, -6.45964093e-01, 1.57079633):
        acc = acc * y + jnp.float32(coef)
    return acc * z


def cos_sin(steps, period):
    turn = jnp.bitwise_and(steps, period - 1)
    half = period // 2
    quarter = period // 4
    cosine = half_turn_sine(jnp.abs(turn - half) - quarter, quarter)
    shifted = jnp.bitwise_and(turn - quarter, period - 1)
    sine = half_turn_sine(jnp.abs(shifted - half) - quarter, quarter)
    return cosine, sine


def split_scalar(value, shape):
    hi = lax.reduce_precision(value, 8, 7)
    mid = lax.reduce_precision(value - hi, 8, 7)
    low = value - hi - mid
    lane = lax.broadcasted_iota(jnp.int32, shape, len(shape) - 1)
    zero = jnp.float32(0.0)
    picked = jnp.where(lane == 0, hi, jnp.where(lane == 1, mid, jnp.where(lane == 2, low, zero)))
    row = lax.broadcasted_iota(jnp.int32, shape, len(shape) - 2)
    return jnp.where(row == 0, picked, zero)


def body(start, observed, coverage, class_weight, degree_gain, legendre, order_table):
    blk_count = lax.axis_size("blk")
    quarter_count = lax.axis_size("quarter")
    blk_index = lax.axis_index("blk")
    quarter_index = lax.axis_index("quarter")
    total = blk_count * quarter_count
    slot_count, cycle_pairs, degree_count = legendre.shape
    order_count = order_table.shape[0]
    funcs, cycle_local, lon_local = observed.shape
    lon_total = lon_local * quarter_count
    half_lon = lon_local // 2
    rows = funcs * cycle_local
    lanes = 2 * slot_count
    pad_rows = -(rows + 1) % 16 + 1
    scale = lon_total ** (-0.5)
    bf16 = jnp.bfloat16
    first_slot = (blk_index * quarter_count + quarter_index) * slot_count
    my_orders = lax.dynamic_slice_in_dim(order_table, first_slot, slot_count)

    tile = min(128, half_lon)
    coarse = jnp.arange(half_lon // tile, dtype=jnp.int32) * tile
    fine = 2 * jnp.arange(tile, dtype=jnp.int32) + 1
    cos_a, sin_a = cos_sin(order_table[:, None] * (2 * coarse)[None, :], 2 * lon_total)
    cos_b, sin_b = cos_sin(order_table[:, None] * fine[None, :], 2 * lon_total)
    centre = 2 * lon_local * quarter_index + (lon_local - 1)
    cos_c, sin_c = cos_sin(order_table * centre, 2 * lon_total)
    cos_a, sin_a, cos_b, sin_b, cos_c, sin_c = lax.optimization_barrier(
        (cos_a, sin_a, cos_b, sin_b, cos_c, sin_c)
    )
    cos_table = jnp.concatenate(
        [cos_a[:, i : i + 1] * cos_b - sin_a[:, i : i + 1] * sin_b for i in range(coarse.shape[0])], 1
    ).astype(bf16)
    sin_table = jnp.concatenate(
        [sin_a[:, i : i + 1] * cos_b + cos_a[:, i : i + 1] * sin_b for i in range(coarse.shape[0])], 1
    ).astype(bf16)
    fused = lanes == 128 and 2 * rows == 16 and pad_rows == rows
    if fused:
        table = jnp.concatenate(
            [
                cos_table.reshape(total, slot_count, half_lon),
                sin_table.reshape(total, slot_count, half_lon),
            ],
            1,
        ).reshape(total * lanes, half_lon)
        cos_c = cos_c.reshape(total, 1, slot_count)
        sin_c = sin_c.reshape(total, 1, slot_count)
        cos_rot = jnp.concatenate([cos_c, cos_c], 2)
        sin_rot = jnp.concatenate([sin_c, -sin_c], 2)

    pair_index = blk_index * (cycle_local // 2) + jnp.arange(cycle_local // 2, dtype=jnp.int32)
    theta = (pair_index.astype(jnp.float32) + 0.5) * (math.pi / (2 * cycle_pairs))
    area = jnp.repeat(jnp.sin(theta), 2)
    classes = jnp.arange(1, class_weight.shape[1] + 1, dtype=jnp.int32)
    matched = coverage[..., None] == classes
    cell_weight = jnp.sum(jnp.where(matched, class_weight[:, None, None, :], 0.0), -1)
    weight = (cell_weight * area[None, :, None]).reshape(rows, lon_local)

    def fold(grid):
        return grid[:, half_lon:], jnp.flip(grid[:, :half_lon], 1)

    observed_plus, observed_minus = fold(observed.reshape(rows, lon_local))
    weight_plus, weight_minus = fold(weight)
    precondition = 1.0 / (jnp.arange(degree_count, dtype=jnp.int32).astype(jnp.float32) + 1.0)

    degrees = jnp.arange(degree_count, dtype=jnp.int32)
    even_mask = ((degrees[None, :] + my_orders[:, None]) % 2 == 0)[:, None, None, :]

    def to_messages(coefficients, partial):
        scaled = degree_gain[None, :, None, :] * coefficients[:, None]
        zeros = jnp.zeros_like(scaled)
        parity = jnp.stack(
            [jnp.where(even_mask, scaled, zeros), jnp.where(even_mask, zeros, scaled)], 1
        ).astype(bf16)
        parts = jnp.einsum("sjl,stfcl->tjfcs", legendre, parity, preferred_element_type=jnp.float32)
        spectra = jnp.stack([parts[0] + parts[1], parts[0] - parts[1]], 1)
        spectra = spectra.reshape(blk_count, cycle_local, funcs, lanes).transpose(0, 2, 1, 3)
        spectra = spectra.reshape(blk_count, rows, lanes)
        tail = jnp.broadcast_to(split_scalar(partial, (pad_rows, lanes)), (blk_count, pad_rows, lanes))
        return jnp.concatenate([spectra, tail], 1).astype(bf16)

    def to_grid(coefficients, partial):
        messages = to_messages(coefficients, partial)
        arrived = exchange(messages, blk_count, quarter_count, True).astype(jnp.float32)
        summed = jnp.sum(arrived[:, rows:])
        spectra = arrived[:, :rows].reshape(total, rows, 2, slot_count).transpose(2, 1, 0, 3)
        spectra = spectra.reshape(2, rows, order_count)
        real = (spectra[0] * cos_c + spectra[1] * sin_c).astype(bf16)
        imag = (spectra[1] * cos_c - spectra[0] * sin_c).astype(bf16)
        even = scale * jnp.dot(real, cos_table, preferred_element_type=jnp.float32)
        odd = scale * jnp.dot(imag, sin_table, preferred_element_type=jnp.float32)
        return even + odd, even - odd, summed

    def to_orders(plus, minus, partial):
        contract = (((1,), (1,)), ((), ()))
        even = lax.dot_general(
            (plus + minus).astype(bf16), cos_table, contract, preferred_element_type=jnp.float32
        )
        odd = lax.dot_general(
            (plus - minus).astype(bf16), sin_table, contract, preferred_element_type=jnp.float32
        )
        real = scale * (even * cos_c - odd * sin_c)
        imag = scale * (even * sin_c + odd * cos_c)
        shares = jnp.stack([real, imag], 1).reshape(rows, 2, total, slot_count).transpose(2, 0, 1, 3)
        shares = shares.reshape(total, rows, lanes)
        tail = jnp.broadcast_to(split_scalar(partial, (pad_rows, lanes)), (total, pad_rows, lanes))
        messages = jnp.concatenate([shares, tail], 1).astype(bf16)
        arrived = exchange(messages, blk_count, quarter_count, False).astype(jnp.float32)
        summed = jnp.sum(arrived[:, rows:])
        returned = jnp.sum(arrived[:, :rows].reshape(blk_count, quarter_count, rows, lanes), 1)
        return to_coefficients(returned), summed

    def to_coefficients(returned):
        returned = returned.reshape(blk_count, funcs, cycle_local // 2, 2, 2, slot_count)
        north, south = returned[:, :, :, 0], returned[:, :, :, 1]
        combined = jnp.stack([north + south, north - south], 0).astype(bf16)
        combined = combined.transpose(5, 0, 4, 2, 1, 3).reshape(slot_count, 2, 2, funcs, cycle_pairs)
        parts = jnp.einsum("sjl,sucfj->sucfl", legendre, combined, preferred_element_type=jnp.float32)
        picked = jnp.where(even_mask, parts[:, 0], parts[:, 1])
        return jnp.sum(degree_gain[None, None, :, :] * picked, 2)

    zero = jnp.float32(0.0)
    one = jnp.float32(1.0)
    solution = start
    if fused:
        stacked_weight = jnp.concatenate([weight_plus, weight_minus], 0)
        image = jnp.concatenate([observed_plus, observed_minus], 0)

        def stage(factors, coefficients, partial, old):
            params = jnp.broadcast_to(jnp.stack(factors + [zero] * 4)[:, None], (8, lanes))
            returned, image, sums = grid_stage(
                params, to_messages(coefficients, partial), old, stacked_weight,
                cos_rot, sin_rot, table, blk_count, quarter_count, scale,
            )
            return to_coefficients(returned), image, sums[0, 0], sums[1, 0]

        gradient, _, _, _ = stage([-one, one, zero, one], start, zero, image)
        direction = energy = None
        for iteration in range(ITERS):
            scaled_grad = precondition * gradient
            factors = [one, zero, zero, one] if iteration == 0 else [one, zero, one, energy]
            change, image, energy_next, curvature = stage(
                factors, scaled_grad, jnp.sum(gradient * scaled_grad), image
            )
            if iteration == 0:
                direction = scaled_grad
            else:
                direction = scaled_grad + energy_next / energy * direction
            energy = energy_next
            step_size = energy / curvature
            solution = solution + step_size * direction
            gradient = gradient - step_size * change
        return (solution, gradient)
    plus, minus, _ = to_grid(start, zero)
    gradient, _ = to_orders(
        weight_plus * (observed_plus - plus), weight_minus * (observed_minus - minus), zero
    )
    direction = energy = image = None
    for iteration in range(ITERS):
        scaled_grad = precondition * gradient
        plus, minus, energy_next = to_grid(scaled_grad, jnp.sum(gradient * scaled_grad))
        if iteration == 0:
            direction = scaled_grad
        else:
            ratio = energy_next / energy
            direction = scaled_grad + ratio * direction
            plus = plus + ratio * image[0]
            minus = minus + ratio * image[1]
        image = (plus, minus)
        energy = energy_next
        weighted_plus, weighted_minus = weight_plus * plus, weight_minus * minus
        partial = jnp.sum(weighted_plus * plus + weighted_minus * minus)
        change, curvature = to_orders(weighted_plus, weighted_minus, partial)
        step_size = energy / curvature
        solution = solution + step_size * direction
        gradient = gradient - step_size * change
    return (solution, gradient)


def solution(mesh):
    return jax.shard_map(
        body,
        mesh=mesh,
        in_specs=(
            P(("blk", "quarter"), None, None),
            P(None, "blk", "quarter"),
            P(None, "blk", "quarter"),
            P(),
            P(),
            P(("blk", "quarter"), None, None),
            P(),
        ),
        out_specs=(P(("blk", "quarter"), None, None), P(("blk", "quarter"), None, None)),
        check_vma=False,
    )
```

profile of v0, /device:TPU:0, one launch (start us, length us, event | category | flops | bytes accessed | tf_op | source)
XLA Modules:
  0.0 144.4 jit_solution(5618028876700754220)
XLA Ops:
  0.7 0.9 add_multiply_fusion.4
  1.5 2.2 %add_multiply_fusion = (f32[2048,128]{1,0:T(8,128)S(1)}, f32[2048,128]{1,0:T(8,128)S(1)}) fusion(s32[128]{0:T(128)S(1)} %multiply_add_fusion.1, s32[2048]{0:T(1024)} %param.13), kind=kLoop, calls=%fused_computation.56 | loop fusion | flops 9961472 | bytes 2105856 | tf_op jit(solution)/shard_map/mul | solution.py:220
  3.7 0.9 add_multiply_fusion.2
  4.7 2.8 %subtract_convert_fusion.3 = (bf16[2048,128]{1,0:T(8,128)(2,1)S(1)}, bf16[2048,128]{1,0:T(8,128)(2,1)S(1)}, bf16[2048,128]{1,0:T(8,128)(2,1)S(1)}, bf16[2048,128...) fusion(f32[2048,128]{1,0:T(8,128)S(1)} %get-tuple-element.19, ...), kind=kLoop, calls=%fused_computation.55 | loop fusion | flops 8388608 | bytes 6356992 | tf_op jit(solution)/shard_map/convert.47
  7.5 2.8 %maximum_maximum_fusion = bf16[32,128,512]{2,1,0:T(8,128)(2,1)} fusion(bf16[32,64,128]{2,1,0:T(8,128)(2,1)S(1)} %bitcast.142, bf16[32,64,128]{2,1,0:T(8,128)(2,1)S(1)} %bitcast.144, bf16[32,64,128]{2,1,0:T(8,128)(2,1)S(1)} %bitcast.146, bf16[32,64,128]{2,1,0:T(8,128)(2,1)S(1)} %bitcast.141, bf16[32,64,128]{2,1,0:T(8,128)(2,1)S(1)} %bitcast.143, ...), kind=kLoop, calls=%fused_computation.28 | loop fusion | flops 33554432 | bytes 8388608 | tf_op jit(solution)/shard_map/concatenate | solution.py:281
  10.3 0.8 dynamic_slice.3
  11.1 0.3 fusion.34
  11.5 2.5 %fusion = (bf16[64,1,4,2,2048]{4,2,3,1,0:T(4,128)(2,1)S(1)}, bf16[64,1,4,2,2048]{4,2,3,1,0:T(4,128)(2,1)S(1)}) fusion(f32[64,2,2048]{2,1,0:T(2,128)S(1)} %copy-done.5, f32[4,2048]{1,0:T(4,128)S(1)} %copy-done.7, pred[64,2048]{1,0:T(8,128)(4,1)S(1)} %fusion.34), kind=kLoop, calls=%fused_computation.6 | loop fusion | flops 5242880 | bytes 5406720 | tf_op jit(solution)/shard_map/convert.56
  14.0 3.1 %fusion.17 = f32[64,2,4,2,8]{4,2,3,1,0:T(4,128)S(1)} fusion(bf16[64,1,4,2,2048]{4,2,3,1,0:T(4,128)(2,1)S(1)} %get-tuple-element.47, bf16[64,1,4,2,2048]{4,2,3,1,0:T(4,128)(2,1)S(1)} %get-tuple-element.46, bf16[64,8,2048]{2,1,0:T(8,128)(2,1)S(1)} %copy-done), kind=kOutput, calls=%fused_computation.33 | convolution fusion | flops 41943040 | bytes 6324224 | tf_op jit(solution)/shard_map/sjl,stfcl->tjfcs/dot_general | solution.py:317
  17.2 0.2 copy.95
  18.3 0.3 rev.8
  18.7 0.3 rev.7
  19.1 2.2 %copy-done.1 = bf16[32,128,512]{2,1,0:T(8,128)(2,1)S(1)} copy-done((bf16[32,128,512]{2,1,0:T(8,128)(2,1)S(1)}, bf16[32,128,512]{2,1,0:T(8,128)(2,1)}, u32[]{:S(2)}) %copy-start.1) | copy-done | bytes 4194328
  21.3 20.0 %grid_stage.3 = (f32[8,8,128]{2,1,0:T(8,128)S(1)}, f32[16,512]{1,0:T(8,128)}, f32[8,128]{1,0:T(8,128)}) custom-call(f32[8,128]{1,0:T(8,128)S(1)} %broadcast_in_dim.132.params_ref, bf16[8,16,128]{2,1,0:T(8,128)(2,1)S(1)} %concatenate.85.send_ref, f32[16,512]{1,0:T(8,128)S(1)} %get-tuple-element.96.old_ref, f32[16,512]{1,0:T(8,128)S(1)} %get-tuple-element.97.weight_ref, ...), custom_call_target="tpu_custom_call" | custom-call | tf_op jit(solution)/shard_map/grid_stage/pallas_call | solution.py:190
  41.4 0.2 copy.127
  41.6 0.2 copy.128
  41.9 1.3 fusion.24
  43.2 4.7 %fusion.14 = f32[64,2,2048]{2,1,0:T(2,128)S(1)} fusion(f32[64,2,2,4,2048]{4,3,2,1,0:T(4,128)S(1)} %fusion.24, f32[4,2048]{1,0:T(4,128)S(1)} %copy-done.7, pred[64,2048]{1,0:T(8,128)(4,1)S(1)} %fusion.34), kind=kLoop, calls=%fused_computation.25 | loop fusion | flops 2883584 | bytes 9601024 | tf_op jit(solution)/shard_map/reduce_sum | solution.py:362
  47.9 1.7 %broadcast_multiply_fusion.1 = (f32[64,2,2048]{2,1,0:T(2,128)S(1)}, f32[]{:T(128)}) fusion(f32[64,2,2048]{2,1,0:T(2,128)S(1)} %fusion.14, f32[2048]{0:T(1024)S(1)} %add_divide_fusion), kind=kLoop, calls=%fused_computation.77 | loop fusion | flops 786431 | bytes 2105348 | tf_op jit(solution)/shard_map/mul | solution.py:382
  49.6 2.5 %fusion.2 = (bf16[64,1,4,2,2048]{4,2,3,1,0:T(4,128)(2,1)S(1)}, bf16[64,1,4,2,2048]{4,2,3,1,0:T(4,128)(2,1)S(1)}) fusion(f32[64,2,2048]{2,1,0:T(2,128)S(1)} %get-tuple-element.48, f32[4,2048]{1,0:T(4,128)S(1)} %copy-done.7, pred[64,2048]{1,0:T(8,128)(4,1)S(1)} %fusion.34), kind=kLoop, calls=%fused_computation.8 | loop fusion | flops 5242880 | bytes 5406720 | tf_op jit(solution)/shard_map/convert.26
  52.2 3.8 %fusion.16 = f32[64,2,4,2,8]{4,2,3,1,0:T(4,128)} fusion(bf16[64,1,4,2,2048]{4,2,3,1,0:T(4,128)(2,1)S(1)} %get-tuple-element.45, bf16[64,1,4,2,2048]{4,2,3,1,0:T(4,128)(2,1)S(1)} %get-tuple-element.44, bf16[64,8,2048]{2,1,0:T(8,128)(2,1)S(1)} %copy-done), kind=kOutput, calls=%fused_computation.32 | convolution fusion | flops 41943040 | bytes 6324224 | tf_op jit(solution)/shard_map/sjl,stfcl->tjfcs/dot_general | solution.py:317
  56.0 1.3 copy.103
  61.2 0.6 copy-done.11
  61.7 1.4 select_convert_fusion.1
  63.2 2.2 %copy-done.2 = bf16[32,128,512]{2,1,0:T(8,128)(2,1)S(1)} copy-done((bf16[32,128,512]{2,1,0:T(8,128)(2,1)S(1)}, bf16[32,128,512]{2,1,0:T(8,128)(2,1)}, u32[]{:S(2)}) %copy-start.2) | copy-done | bytes 4194328
  65.4 14.9 %grid_stage.4 = (f32[8,8,128]{2,1,0:T(8,128)S(1)}, f32[16,512]{1,0:T(8,128)S(1)}, f32[8,128]{1,0:T(8,128)S(1)}) custom-call(f32[8,128]{1,0:T(8,128)S(1)} %broadcast_in_dim.129.params_ref, bf16[8,16,128]{2,1,0:T(8,128)(2,1)S(1)} %pad_maximum_fusion.8.send_ref, f32[16,512]{1,0:T(8,128)S(1)} %get-tuple-element.96.old_ref, ...), custom_call_target="tpu_custom_call" | custom-call | tf_op jit(solution)/shard_map/grid_stage/pallas_call | solution.py:190
  80.3 0.5 fusion.72
  82.3 0.8 copy.130
  83.2 0.8 copy.131
  84.0 1.1 fusion.44
  85.1 1.3 fusion.20
  86.5 4.7 %fusion.11 = f32[64,2,2048]{2,1,0:T(2,128)S(1)} fusion(f32[64,2,2,4,2048]{4,3,2,0,1:T(4,128)S(1)} %fusion.20, f32[4,2048]{1,0:T(4,128)S(1)} %copy-done.7, pred[64,2048]{1,0:T(8,128)(4,1)S(1)} %fusion.34), kind=kLoop, calls=%fused_computation.20 | loop fusion | flops 2883584 | bytes 9601024 | tf_op jit(solution)/shard_map/reduce_sum | solution.py:362
  91.2 2.2 %broadcast_multiply_fusion = (f32[64,2,2048]{2,1,0:T(2,128)S(1)}, f32[64,2,2048]{2,1,0:T(2,128)}) fusion(f32[2048]{0:T(1024)S(1)} %add_divide_fusion, f32[64,2,2048]{2,1,0:T(2,128)S(1)} %fusion.14, f32[64,2,2048]{2,1,0:T(2,128)S(1)} %fusion.11, f32[]{:T(128)} %bitcast.32), kind=kLoop, calls=%fused_computation.76 | loop fusion | flops 786432 | bytes 4202500 | tf_op jit(solution)/shard_map/mul | solution.py:382
  93.4 2.5 %fusion.4 = (bf16[64,1,4,2,2048]{4,2,3,1,0:T(4,128)(2,1)S(1)}, bf16[64,1,4,2,2048]{4,2,3,1,0:T(4,128)(2,1)S(1)}) fusion(f32[64,2,2048]{2,1,0:T(2,128)S(1)} %get-tuple-element.26, f32[4,2048]{1,0:T(4,128)S(1)} %copy-done.7, pred[64,2048]{1,0:T(8,128)(4,1)S(1)} %fusion.34), kind=kLoop, calls=%fused_computation.10 | loop fusion | flops 5242880 | bytes 5406720 | tf_op jit(solution)/shard_map/convert.12
  95.9 3.8 %fusion.15 = f32[64,2,4,2,8]{4,2,3,1,0:T(4,128)} fusion(bf16[64,1,4,2,2048]{4,2,3,1,0:T(4,128)(2,1)S(1)} %get-tuple-element.43, bf16[64,1,4,2,2048]{4,2,3,1,0:T(4,128)(2,1)S(1)} %get-tuple-element.42, bf16[64,8,2048]{2,1,0:T(8,128)(2,1)S(1)} %copy-done), kind=kOutput, calls=%fused_computation.31 | convolution fusion | flops 41943040 | bytes 6324224 | tf_op jit(solution)/shard_map/sjl,stfcl->tjfcs/dot_general | solution.py:317
  99.7 1.3 copy.112
  101.2 2.9 %multiply_reduce_fusion = f32[]{:T(128)} fusion(f32[64,2,2048]{2,1,0:T(2,128)} %get-tuple-element.27, f32[2048]{0:T(1024)S(1)} %add_divide_fusion), kind=kLoop, calls=%fused_computation.45 | loop fusion | flops 786431 | bytes 1056772 | tf_op jit(solution)/shard_map/reduce_sum | solution.py:385
  107.7 1.3 select_convert_fusion
  109.0 0.7 stack.70
  109.8 2.2 %copy-done.3 = bf16[32,128,512]{2,1,0:T(8,128)(2,1)S(1)} copy-done((bf16[32,128,512]{2,1,0:T(8,128)(2,1)S(1)}, bf16[32,128,512]{2,1,0:T(8,128)(2,1)}, u32[]{:S(2)}) %copy-start.3) | copy-done | bytes 4194328
  112.0 16.8 %grid_stage.5 = (f32[8,8,128]{2,1,0:T(8,128)S(1)}, f32[16,512]{1,0:T(8,128)}, f32[8,128]{1,0:T(8,128)S(1)}) custom-call(f32[8,128]{1,0:T(8,128)S(1)} %broadcast_in_dim.141.params_ref, bf16[8,16,128]{2,1,0:T(8,128)(2,1)S(1)} %pad_maximum_fusion.9.send_ref, f32[16,512]{1,0:T(8,128)S(1)} %get-tuple-element.23.old_ref, ...), custom_call_target="tpu_custom_call" | custom-call | tf_op jit(solution)/shard_map/grid_stage/pallas_call | solution.py:190
  128.7 0.6 fusion.71
  132.2 0.8 copy.132
  133.0 0.8 copy.133
  133.8 1.1 fusion.46
  135.0 1.3 fusion.18
  136.3 4.7 %fusion.8 = f32[64,2,2048]{2,1,0:T(2,128)S(1)} fusion(f32[64,2,2,4,2048]{4,3,2,0,1:T(4,128)S(1)} %fusion.18, f32[4,2048]{1,0:T(4,128)S(1)} %copy-done.7, pred[64,2048]{1,0:T(8,128)(4,1)S(1)} %fusion.34), kind=kLoop, calls=%fused_computation.15 | loop fusion | flops 2883584 | bytes 9601024 | tf_op jit(solution)/shard_map/reduce_sum | solution.py:362
  141.1 3.4 %multiply_subtract_fusion = (f32[64,2,2048]{2,1,0:T(2,128)}, f32[64,2,2048]{2,1,0:T(2,128)}) fusion(f32[64,2,2048]{2,1,0:T(2,128)S(1)} %copy-done.4, f32[64,2,2048]{2,1,0:T(2,128)S(1)} %fusion.8, f32[]{:T(128)} %bitcast.46, f32[]{:T(128)} %bitcast.47, f32[64,2,2048]{2,1,0:T(2,128)S(1)} %copy-done.6, f32[64,2,2048]{2,1,0:T(2,128)S(1)} %fusion.14, ...), kind=kLoop, calls=%fused_computation.43 | loop fusion | flops 2621440 | bytes 6299660 | tf_op jit(solution)/shard_map/sub | solution.py:394
  (83 shorter events, 2.1 us)
Async XLA Ops:
  0.6 13.4 %copy-start = (bf16[64,8,2048]{2,1,0:T(8,128)(2,1)S(1)}, bf16[64,8,2048]{2,1,0:T(8,128)(2,1)}, u32[]{:S(2)}) copy-start(bf16[64,8,2048]{2,1,0:T(8,128)(2,1)} %param.12) | copy-start | bytes 6291460
  7.5 3.9 %copy-start.5 = (f32[64,2,2048]{2,1,0:T(2,128)S(1)}, f32[64,2,2048]{2,1,0:T(2,128)}, u32[]{:S(2)}) copy-start(f32[64,2,2048]{2,1,0:T(2,128)} %param.7) | copy-start | bytes 3145732
  7.5 3.9 %copy-start.7 = (f32[4,2048]{1,0:T(4,128)S(1)}, f32[4,2048]{1,0:T(4,128)}, u32[]{:S(2)}) copy-start(f32[4,2048]{1,0:T(4,128)} %param.11) | copy-start | bytes 98308
  14.0 4.1 %copy-start.8 = (s32[4,2,1024]{2,1,0:T(2,128)S(1)}, s32[4,2,1024]{2,1,0:T(2,128)}, u32[]{:S(2)}) copy-start(s32[4,2,1024]{2,1,0:T(2,128)} %param.9) | copy-start | bytes 98308
  14.0 4.1 %copy-start.10 = (f32[4,4]{1,0:T(4,128)S(1)}, f32[4,4]{1,0:T(4,128)}, u32[]{:S(2)}) copy-start(f32[4,4]{1,0:T(4,128)} %param.10) | copy-start | bytes 196
  14.0 4.6 %copy-start.9 = (f32[4,2,1024]{2,1,0:T(2,128)S(1)}, f32[4,2,1024]{2,1,0:T(2,128)}, u32[]{:S(2)}) copy-start(f32[4,2,1024]{2,1,0:T(2,128)} %param.8) | copy-start | bytes 98308
  14.0 5.0 %copy-start.14 = (f32[8]{0:T(128)S(1)}, f32[8]{0:T(128)}, u32[]{:S(2)}) copy-start(f32[8]{0:T(128)} %constant.47.clone.1) | copy-start | bytes 100
  19.1 2.2 %copy-start.1 = (bf16[32,128,512]{2,1,0:T(8,128)(2,1)S(1)}, bf16[32,128,512]{2,1,0:T(8,128)(2,1)}, u32[]{:S(2)}) copy-start(bf16[32,128,512]{2,1,0:T(8,128)(2,1)} %maximum_maximum_fusion) | copy-start | bytes 12582916
  52.1 11.0 %copy-start.13 = (f32[8]{0:T(128)S(1)}, f32[8]{0:T(128)}, u32[]{:S(2)}) copy-start(f32[8]{0:T(128)} %constant.36.clone.1) | copy-start | bytes 100
  61.1 0.6 copy-start.11
  63.2 2.2 %copy-start.2 = (bf16[32,128,512]{2,1,0:T(8,128)(2,1)S(1)}, bf16[32,128,512]{2,1,0:T(8,128)(2,1)}, u32[]{:S(2)}) copy-start(bf16[32,128,512]{2,1,0:T(8,128)(2,1)} %maximum_maximum_fusion) | copy-start | bytes 12582916
  95.9 11.8 %copy-start.12 = (pred[8]{0:T(512)(128)(4,1)S(1)}, pred[8]{0:T(512)(128)(4,1)}, u32[]{:S(2)}) copy-start(pred[8]{0:T(512)(128)(4,1)} %copy-done.11) | copy-start | bytes 28
  109.8 2.2 %copy-start.3 = (bf16[32,128,512]{2,1,0:T(8,128)(2,1)S(1)}, bf16[32,128,512]{2,1,0:T(8,128)(2,1)}, u32[]{:S(2)}) copy-start(bf16[32,128,512]{2,1,0:T(8,128)(2,1)} %maximum_maximum_fusion) | copy-start | bytes 12582916
  136.3 4.8 %copy-start.4 = (f32[64,2,2048]{2,1,0:T(2,128)S(1)}, f32[64,2,2048]{2,1,0:T(2,128)}, u32[]{:S(2)}) copy-start(f32[64,2,2048]{2,1,0:T(2,128)} %get-tuple-element.27) | copy-start | bytes 3145732
  136.3 4.8 %copy-start.6 = (f32[64,2,2048]{2,1,0:T(2,128)S(1)}, f32[64,2,2048]{2,1,0:T(2,128)}, u32[]{:S(2)}) copy-start(f32[64,2,2048]{2,1,0:T(2,128)} %param.7) | copy-start | bytes 3145732
where the time goes:
time: 145 us; the launch traced here: 144 us
  Pallas kernels  51.7 us (36%)
  other arithmetic  47.1 us (32%)
  local copies, waits for them, and re-layouts  18.4 us (13%)
  matrix products  14.7 us (10%)
  between operations  12.5 us (9%)
    pallas_call x3, Pallas kernels, grid_stage(): pl.pallas_call(functools.partial(grid_kernel, blk_count, quarter_count, s...  51.7 us
    reduce_sum x3, other arithmetic, to_coefficients(): return jnp.sum(degree_gain[None, None, :, :] * picked, 2)  14.1 us
    another operation x9, other arithmetic  13 us
    unnamed x36, local copies, waits for them, and re-layouts  10.9 us
    dot_general x3, matrix products, to_messages(): jnp.einsum('sjl,stfcl->tjfcs', legendre, parity, preferred_element_type=j...  10.7 us
    dot_general x3, matrix products, to_coefficients(): jnp.einsum('sjl,sucfj->sucfl', legendre, combined, preferred_element_type...  4 us
    mul x3, other arithmetic, half_turn_sine(): return acc * z  3.93 us
    mul x2, other arithmetic, body(): scaled_grad = precondition * gradient  3.88 us

commit v1 on v0

--- a/solution.py
+++ b/solution.py
@@ -211,6 +211,116 @@
     )(params, messages, old, weight, cos_rot, sin_rot, table)
 
 
+def synth_kernel(
+    blk_count, values_ref, factor_ref, gain_ref, sign_ref, legendre_ref, message_ref, right_ref, rows_ref
+):
+    lanes, degree_count = values_ref.shape
+    slot_count = lanes // 2
+    funcs = gain_ref.shape[0]
+    values = values_ref[...]
+    scaled = factor_ref[...] * values
+    lane_sign = 1 - 2 * (lax.broadcasted_iota(jnp.int32, (1, degree_count), 1) % 2)
+    sign = sign_ref[...] * lane_sign.astype(jnp.float32)
+    partial = jnp.sum(values * scaled, 0, keepdims=True)
+    partial = sum(partial[:, i : i + lanes] for i in range(0, degree_count, lanes))
+    high = partial.astype(jnp.bfloat16).astype(jnp.float32)
+    middle = (partial - high).astype(jnp.bfloat16).astype(jnp.float32)
+    low = partial - high - middle
+    row = lax.broadcasted_iota(jnp.int32, (8, lanes), 0)
+    tail = jnp.where(row == 0, high, jnp.where(row == 1, middle, jnp.where(row == 2, low, 0.0)))
+    slot = lax.broadcasted_iota(jnp.int32, (slot_count, 2 * lanes), 0)
+    lane = lax.broadcasted_iota(jnp.int32, (slot_count, 2 * lanes), 1)
+    own = slot == lane % slot_count
+    for f in range(funcs):
+        north = gain_ref[f : f + 1, :] * scaled
+        right_ref[:lanes] = north.astype(jnp.bfloat16)
+        right_ref[lanes:] = (north * sign).astype(jnp.bfloat16)
+        parts = lax.dot_general(
+            legendre_ref[...], right_ref[...], (((1,), (1,)), ((), ())),
+            preferred_element_type=jnp.float32,
+        )
+        for j in range(blk_count):
+            part = parts[j * slot_count : (j + 1) * slot_count]
+            kept = jnp.sum(jnp.where(own, part, 0.0), 0, keepdims=True)
+            rows_ref[j, 2 * f : 2 * f + 1, :] = kept[:, :lanes]
+            rows_ref[j, 2 * f + 1 : 2 * f + 2, :] = kept[:, lanes:]
+    for j in range(blk_count):
+        message_ref[j] = jnp.concatenate([rows_ref[j], tail], 0).astype(jnp.bfloat16)
+
+
+def synth_stage(values, factor, gains, sign, legendre_rows, blk_count):
+    lanes, degree_count = values.shape
+    rows = 2 * gains.shape[0]
+    return pl.pallas_call(
+        functools.partial(synth_kernel, blk_count),
+        out_shape=jax.ShapeDtypeStruct((blk_count, 2 * rows, lanes), jnp.bfloat16),
+        in_specs=[pl.BlockSpec(memory_space=pltpu.VMEM)] * 5,
+        out_specs=pl.BlockSpec(memory_space=pltpu.VMEM),
+        scratch_shapes=[
+            pltpu.VMEM((2 * lanes, degree_count), jnp.bfloat16),
+            pltpu.VMEM((blk_count, rows, lanes), jnp.float32),
+        ],
+        compiler_params=pltpu.CompilerParams(vmem_limit_bytes=24 << 20),
+        name="synth_stage",
+    )(values, factor, gains, sign, legendre_rows)
+
+
+def adjoint_kernel(blk_count, returned_ref, gain_ref, sign_ref, legendre_ref, change_ref, left_ref):
+    lanes, degree_count = change_ref.shape
+    slot_count = lanes // 2
+    funcs = gain_ref.shape[0]
+    slot = lax.broadcasted_iota(jnp.int32, (slot_count, lanes), 0)
+    lane = lax.broadcasted_iota(jnp.int32, (slot_count, lanes), 1)
+    own = slot == lane % slot_count
+    first = lax.broadcasted_iota(jnp.int32, (1, lanes), 1) < slot_count
+    for a in range(blk_count // 2):
+        near, far = returned_ref[2 * a], returned_ref[2 * a + 1]
+        near_turned, far_turned = pltpu.roll(near, slot_count, 1), pltpu.roll(far, slot_count, 1)
+        parts = (jnp.where(first, near, far_turned), jnp.where(first, near_turned, far))
+        for c in range(2):
+            for f in range(funcs):
+                north = parts[c][2 * f : 2 * f + 1]
+                south = parts[c][2 * f + 1 : 2 * f + 2]
+                for u, hemis in enumerate((north + south, north - south)):
+                    at = ((c * funcs + f) * 2 + u) * slot_count
+                    left_ref[at : at + slot_count, a * lanes : (a + 1) * lanes] = jnp.where(
+                        own, hemis, 0.0
+                    ).astype(jnp.bfloat16)
+    width = 256
+    even_lane = lax.broadcasted_iota(jnp.int32, (slot_count, width), 1) % 2 == 0
+    even_order = sign_ref[:slot_count, :] > 0.0
+    even = even_lane == even_order
+    for at in range(0, degree_count, width):
+        parts = jnp.dot(
+            left_ref[...], legendre_ref[:, at : at + width], preferred_element_type=jnp.float32
+        )
+        for c in range(2):
+            total = None
+            for f in range(funcs):
+                base = (c * funcs + f) * 2 * slot_count
+                picked = jnp.where(
+                    even, parts[base : base + slot_count],
+                    parts[base + slot_count : base + 2 * slot_count],
+                )
+                term = gain_ref[f : f + 1, at : at + width] * picked
+                total = term if f == 0 else total + term
+            change_ref[c * slot_count : (c + 1) * slot_count, at : at + width] = total
+
+
+def adjoint_stage(returned, gains, sign, legendre_rows):
+    blk_count, rows, lanes = returned.shape
+    degree_count = legendre_rows.shape[1]
+    return pl.pallas_call(
+        functools.partial(adjoint_kernel, blk_count),
+        out_shape=jax.ShapeDtypeStruct((lanes, degree_count), jnp.float32),
+        in_specs=[pl.BlockSpec(memory_space=pltpu.VMEM)] * 4,
+        out_specs=pl.BlockSpec(memory_space=pltpu.VMEM),
+        scratch_shapes=[pltpu.VMEM((rows * lanes, legendre_rows.shape[0]), jnp.bfloat16)],
+        compiler_params=pltpu.CompilerParams(vmem_limit_bytes=24 << 20),
+        name="adjoint_stage",
+    )(returned, gains, sign, legendre_rows)
+
+
 def half_turn_sine(phase, quarter_turn):
     z = phase.astype(jnp.float32) * (1.0 / quarter_turn)
     y = z * z
@@ -276,7 +386,7 @@
     sin_table = jnp.concatenate(
         [sin_a[:, i : i + 1] * cos_b + cos_a[:, i : i + 1] * sin_b for i in range(coarse.shape[0])], 1
     ).astype(bf16)
-    fused = lanes == 128 and 2 * rows == 16 and pad_rows == rows
+    fused = lanes == 128 and rows == 8 and cycle_local == 2 and cycle_pairs == blk_count
     if fused:
         table = jnp.concatenate(
             [
@@ -367,23 +477,30 @@
     if fused:
         stacked_weight = jnp.concatenate([weight_plus, weight_minus], 0)
         image = jnp.concatenate([observed_plus, observed_minus], 0)
-
-        def stage(factors, coefficients, partial, old):
+        legendre_rows = legendre.transpose(1, 0, 2).reshape(cycle_pairs * slot_count, degree_count)
+        order_sign = (1 - 2 * (my_orders % 2)).astype(jnp.float32)
+        order_sign = jnp.concatenate([order_sign, order_sign])[:, None]
+        factor = precondition[None, :]
+
+        def stage(factors, coefficients, multiplier, old):
             params = jnp.broadcast_to(jnp.stack(factors + [zero] * 4)[:, None], (8, lanes))
+            messages = synth_stage(
+                coefficients, multiplier, degree_gain, order_sign, legendre_rows, blk_count
+            )
             returned, image, sums = grid_stage(
-                params, to_messages(coefficients, partial), old, stacked_weight,
+                params, messages, old, stacked_weight,
                 cos_rot, sin_rot, table, blk_count, quarter_count, scale,
             )
-            return to_coefficients(returned), image, sums[0, 0], sums[1, 0]
-
-        gradient, _, _, _ = stage([-one, one, zero, one], start, zero, image)
+            change = adjoint_stage(returned, degree_gain, order_sign, legendre_rows)
+            return change, image, sums[0, 0], sums[1, 0]
+
+        solution = start.transpose(1, 0, 2).reshape(lanes, degree_count)
+        gradient, _, _, _ = stage([-one, one, zero, one], solution, jnp.ones_like(factor), image)
         direction = energy = None
         for iteration in range(ITERS):
-            scaled_grad = precondition * gradient
+            scaled_grad = factor * gradient
             factors = [one, zero, zero, one] if iteration == 0 else [one, zero, one, energy]
-            change, image, energy_next, curvature = stage(
-                factors, scaled_grad, jnp.sum(gradient * scaled_grad), image
-            )
+            change, image, energy_next, curvature = stage(factors, gradient, factor, image)
             if iteration == 0:
                 direction = scaled_grad
             else:
@@ -392,7 +509,9 @@
             step_size = energy / curvature
             solution = solution + step_size * direction
             gradient = gradient - step_size * change
-        return (solution, gradient)
+        return tuple(
+            out.reshape(2, slot_count, degree_count).transpose(1, 0, 2) for out in (solution, gradient)
+        )
     plus, minus, _ = to_grid(start, zero)
     gradient, _ = to_orders(
         weight_plus * (observed_plus - plus), weight_minus * (observed_minus - minus), zero

time: 145 us -> 99.6 us (0.69)
  other arithmetic: 47.1 us -> 11.2 us
  Pallas kernels: 51.7 us -> 66.4 us
  matrix products: 14.7 us -> 0 us
  between operations: 12.5 us -> 5.13 us
  local copies, waits for them, and re-layouts: 18.4 us -> 16.4 us
    reduce_sum x4 -> x0, other arithmetic: 17 us -> none  [the longest x3 14.1 us: to_coefficients(): return jnp.sum(degree_gain[None, None, :, :] * picked, 2)]
    dot_general x6 -> x0, matrix products: 14.7 us -> none  [the longest x3 10.7 us: to_messages(): jnp.einsum('sjl,stfcl->tjfcs', legendre, parity, preferred_element_type=j...]
    pallas_call x0 -> x6, Pallas kernels: none -> 14.6 us  [the longest x3 7.31 us: synth_stage(): pl.pallas_call(functools.partial(synth_kernel, blk_count), out_shape=jax....]
    another operation x12 -> x1, other arithmetic: 15.4 us -> 2.84 us
    unnamed x36 -> x28, local copies, waits for them, and re-layouts: 10.9 us -> 6.36 us
    mul x2 -> x0, other arithmetic: 3.88 us -> none  [body(): scaled_grad = precondition * gradient]
    transpose x3 -> x2, local copies, waits for them, and re-layouts: 0.05 us -> 3.38 us  [the longest x1 2.76 us: body(): legendre.transpose(1, 0, 2).reshape(cycle_pairs * slot_count, degree_count)]
    reshape x3 -> x2, local copies, waits for them, and re-layouts: 0.29 us -> 3.56 us  [body(): out.reshape(2, slot_count, degree_count).transpose(1, 0, 2)]
where the time goes in v1:
time: 99.6 us; the launch traced here: 99.1 us
  Pallas kernels  66.4 us (67%)
  local copies, waits for them, and re-layouts  16.4 us (16%)
  other arithmetic  11.2 us (11%)
  between operations  5.13 us (5%)
    pallas_call x3, Pallas kernels, grid_stage(): pl.pallas_call(functools.partial(grid_kernel, blk_count, quarter_count, s...  51.9 us
    pallas_call x3, Pallas kernels, synth_stage(): pl.pallas_call(functools.partial(synth_kernel, blk_count), out_shape=jax....  7.31 us
    pallas_call x3, Pallas kernels, adjoint_stage(): pl.pallas_call(functools.partial(adjoint_kernel, blk_count), out_shape=ja...  7.28 us
    unnamed x28, local copies, waits for them, and re-layouts  6.36 us
    mul x3, other arithmetic, half_turn_sine(): return acc * z  3.78 us
    reshape x2, local copies, waits for them, and re-layouts, body(): out.reshape(2, slot_count, degree_count).transpose(1, 0, 2)  3.56 us
    another operation x1, other arithmetic  2.84 us
    concatenate x1, other arithmetic, body(): jnp.concatenate([cos_table.reshape(total, slot_count, half_lon), sin_tabl...  2.79 us

profile of v1, /device:TPU:0, one launch (start us, length us, event | category | flops | bytes accessed | tf_op | source)
XLA Modules:
  0.0 99.1 jit_solution(7836740246851760284)
XLA Ops:
  0.6 0.7 add_multiply_fusion.4
  1.4 2.2 %add_multiply_fusion = (f32[2048,128]{1,0:T(8,128)S(1)}, f32[2048,128]{1,0:T(8,128)S(1)}) fusion(s32[128]{0:T(128)S(1)} %multiply_add_fusion.1, s32[2048]{0:T(1024)} %param.13), kind=kLoop, calls=%fused_computation.14 | loop fusion | flops 9961472 | bytes 2105856 | tf_op jit(solution)/shard_map/mul | solution.py:330
  3.6 0.9 add_multiply_fusion.2
  4.5 2.8 %subtract_convert_fusion.3 = (bf16[2048,128]{1,0:T(8,128)(2,1)S(1)}, bf16[2048,128]{1,0:T(8,128)(2,1)S(1)}, bf16[2048,128]{1,0:T(8,128)(2,1)S(1)}, bf16[2048,128...) fusion(f32[2048,128]{1,0:T(8,128)S(1)} %get-tuple-element.19, ...), kind=kLoop, calls=%fused_computation.13 | loop fusion | flops 8388608 | bytes 6356992 | tf_op jit(solution)/shard_map/convert.15
  7.3 2.8 %maximum_maximum_fusion = bf16[32,128,512]{2,1,0:T(8,128)(2,1)} fusion(bf16[32,64,128]{2,1,0:T(8,128)(2,1)S(1)} %bitcast.52, bf16[32,64,128]{2,1,0:T(8,128)(2,1)S(1)} %bitcast.54, bf16[32,64,128]{2,1,0:T(8,128)(2,1)S(1)} %bitcast.56, bf16[32,64,128]{2,1,0:T(8,128)(2,1)S(1)} %bitcast.51, bf16[32,64,128]{2,1,0:T(8,128)(2,1)S(1)} %bitcast.53, ...), kind=kLoop, calls=%fused_computation | loop fusion | flops 33554432 | bytes 8388608 | tf_op jit(solution)/shard_map/concatenate | solution.py:391
  10.1 0.1 reshape.109
  10.2 0.1 reshape.108
  10.3 0.1 pad_maximum_fusion.2
  10.5 0.8 fusion.20
  11.2 0.1 maximum_bitcast_fusion
  11.3 0.1 copy.31.sign_ref
  11.4 0.0 copy-start.11
  11.4 0.0 copy-start.10
  11.5 0.0 copy-start.13
  11.5 2.8 %copy.30 = bf16[8,64,2048]{2,1,0:T(8,128)(2,1)S(1)} copy(bf16[8,64,2048]{2,0,1:T(8,128)(2,1)} %bitcast.58) | data formatting | bytes 4194304 | tf_op jit(solution)/shard_map/transpose | solution.py:480
  14.2 0.0 copy-done.8
  14.2 0.6 copy.29
  14.9 0.0 copy-done.7
  14.9 2.4 %synth_stage.3.send_ref = bf16[8,16,128]{2,1,0:T(8,128)(2,1)S(1)} custom-call(f32[128,2048]{1,0:T(8,128)S(1)} %bitcast.47, f32[1,2048]{1,0:T(1,128)S(1)} %broadcast_in_dim.26.factor_ref, f32[4,2048]{1,0:T(4,128)S(1)} %copy-done.7, f32[128,1]{1,0:T(8,128)S(1)} %copy.31.sign_ref, bf16[512,2048]{1,0:T(8,128)(2,1)S(1)} %bitcast.38), custom_call_target="tpu_custom_call" | custom-call | tf_op jit(solution)/shard_map/synth_stage/pallas_call | solution.py:254
  17.3 0.0 copy-start.3
  17.3 1.0 copy-done.3
  18.4 0.0 copy-done.9
  18.4 0.2 select_reduce_fusion
  18.6 0.3 rev.8
  19.0 0.3 rev.7
  19.3 0.1 broadcast_in_dim.25.params_ref
  19.4 2.2 %copy-done = bf16[32,128,512]{2,1,0:T(8,128)(2,1)S(1)} copy-done((bf16[32,128,512]{2,1,0:T(8,128)(2,1)S(1)}, bf16[32,128,512]{2,1,0:T(8,128)(2,1)}, u32[]{:S(2)}) %copy-start) | copy-done | bytes 4194328
  21.6 20.0 %grid_stage.3 = (f32[8,8,128]{2,1,0:T(8,128)S(1)}, f32[16,512]{1,0:T(8,128)}, f32[8,128]{1,0:T(8,128)}) custom-call(f32[8,128]{1,0:T(8,128)S(1)} %broadcast_in_dim.25.params_ref, bf16[8,16,128]{2,1,0:T(8,128)(2,1)S(1)} %synth_stage.3.send_ref, f32[16,512]{1,0:T(8,128)S(1)} %get-tuple-element.68.old_ref, f32[16,512]{1,0:T(8,128)S(1)} %get-tuple-element.69.weight_ref, ...), custom_call_target="tpu_custom_call" | custom-call | tf_op jit(solution)/shard_map/grid_stage/pallas_call | solution.py:190
  41.6 0.0 copy-start.12
  41.6 2.4 %adjoint_stage.3.values_ref = f32[128,2048]{1,0:T(8,128)S(1)} custom-call(f32[8,8,128]{2,1,0:T(8,128)S(1)} %get-tuple-element.20.returned_ref, f32[4,2048]{1,0:T(4,128)S(1)} %copy-done.7, f32[128,1]{1,0:T(8,128)S(1)} %copy.31.sign_ref, bf16[512,2048]{1,0:T(8,128)(2,1)S(1)} %bitcast.39), custom_call_target="tpu_custom_call" | custom-call | tf_op jit(solution)/shard_map/adjoint_stage/pallas_call | solution.py:313
  44.1 2.4 %synth_stage.4.send_ref = bf16[8,16,128]{2,1,0:T(8,128)(2,1)S(1)} custom-call(f32[128,2048]{1,0:T(8,128)S(1)} %adjoint_stage.3.values_ref, f32[1,2048]{1,0:T(1,128)S(1)} %add_divide_fusion.1.factor_ref, f32[4,2048]{1,0:T(4,128)S(1)} %copy-done.7, f32[128,1]{1,0:T(8,128)S(1)} %copy.31.sign_ref, bf16[512,2048]{1,0:T(8,128)(2,1)S(1)} %bitcast.40), custom_call_target="tpu_custom_call" | custom-call | tf_op jit(solution)/shard_map/synth_stage/pallas_call | solution.py:254
  46.5 0.1 broadcast_in_dim.24.params_ref
  46.6 14.9 %grid_stage.4 = (f32[8,8,128]{2,1,0:T(8,128)S(1)}, f32[16,512]{1,0:T(8,128)S(1)}, f32[8,128]{1,0:T(8,128)S(1)}) custom-call(f32[8,128]{1,0:T(8,128)S(1)} %broadcast_in_dim.24.params_ref, bf16[8,16,128]{2,1,0:T(8,128)(2,1)S(1)} %synth_stage.4.send_ref, f32[16,512]{1,0:T(8,128)S(1)} %get-tuple-element.68.old_ref, f32[16,512]{1,0:T(8,128)S(1)} %get-tuple-element.69.weight_ref, ...), custom_call_target="tpu_custom_call" | custom-call | tf_op jit(solution)/shard_map/grid_stage/pallas_call | solution.py:190
  61.5 0.6 fusion.27
  63.4 2.4 %adjoint_stage.4 = f32[128,2048]{1,0:T(8,128)S(1)} custom-call(f32[8,8,128]{2,1,0:T(8,128)S(1)} %get-tuple-element.22.returned_ref, f32[4,2048]{1,0:T(4,128)S(1)} %copy-done.7, f32[128,1]{1,0:T(8,128)S(1)} %copy.31.sign_ref, bf16[512,2048]{1,0:T(8,128)(2,1)S(1)} %bitcast.41), custom_call_target="tpu_custom_call" | custom-call | tf_op jit(solution)/shard_map/adjoint_stage/pallas_call | solution.py:313
  65.9 0.1 multiply_subtract_fusion.1.values_ref
  66.0 2.5 %synth_stage.5.send_ref = bf16[8,16,128]{2,1,0:T(8,128)(2,1)S(1)} custom-call(f32[128,2048]{1,0:T(8,128)S(1)} %multiply_subtract_fusion.1.values_ref, f32[1,2048]{1,0:T(1,128)S(1)} %add_divide_fusion.1.factor_ref, f32[4,2048]{1,0:T(4,128)S(1)} %copy-done.7, f32[128,1]{1,0:T(8,128)S(1)} %copy.31.sign_ref, bf16[512,2048]{1,0:T(8,128)(2,1)S(1)} %bitcast.42), custom_call_target="tpu_custom_call" | custom-call | tf_op jit(solution)/shard_map/synth_stage/pallas_call | solution.py:254
  68.5 0.0 copy-start.5
  68.5 1.0 copy-done.5
  69.5 0.7 stack.3
  70.2 0.1 broadcast_in_dim.52.params_ref
  70.2 2.2 %copy-done.2 = bf16[32,128,512]{2,1,0:T(8,128)(2,1)S(1)} copy-done((bf16[32,128,512]{2,1,0:T(8,128)(2,1)S(1)}, bf16[32,128,512]{2,1,0:T(8,128)(2,1)}, u32[]{:S(2)}) %copy-start.2) | copy-done | bytes 4194328
  72.4 16.9 %grid_stage.5 = (f32[8,8,128]{2,1,0:T(8,128)S(1)}, f32[16,512]{1,0:T(8,128)}, f32[8,128]{1,0:T(8,128)S(1)}) custom-call(f32[8,128]{1,0:T(8,128)S(1)} %broadcast_in_dim.52.params_ref, bf16[8,16,128]{2,1,0:T(8,128)(2,1)S(1)} %synth_stage.5.send_ref, f32[16,512]{1,0:T(8,128)S(1)} %get-tuple-element.23.old_ref, f32[16,512]{1,0:T(8,128)S(1)} %get-tuple-element.69.weight_ref, ...), custom_call_target="tpu_custom_call" | custom-call | tf_op jit(solution)/shard_map/grid_stage/pallas_call | solution.py:190
  89.3 0.6 fusion.26
  92.7 2.4 %adjoint_stage.5 = f32[128,2048]{1,0:T(8,128)S(1)} custom-call(f32[8,8,128]{2,1,0:T(8,128)S(1)} %get-tuple-element.25.returned_ref, f32[4,2048]{1,0:T(4,128)S(1)} %copy-done.7, f32[128,1]{1,0:T(8,128)S(1)} %copy.31.sign_ref, bf16[512,2048]{1,0:T(8,128)(2,1)S(1)} %bitcast.43), custom_call_target="tpu_custom_call" | custom-call | tf_op jit(solution)/shard_map/adjoint_stage/pallas_call | solution.py:313
  95.2 0.4 multiply_subtract_fusion
  95.6 1.8 %copy.41 = f32[2,64,2048]{2,0,1:T(2,128)} copy(f32[2,64,2048]{2,1,0:T(8,128)S(1)} %bitcast.49) | data formatting | bytes 2097152 | tf_op jit(solution)/shard_map/reshape | solution.py:513
  97.4 1.8 %copy.42 = f32[2,64,2048]{2,0,1:T(2,128)} copy(f32[2,64,2048]{2,1,0:T(8,128)S(1)} %bitcast.48) | data formatting | bytes 2097152 | tf_op jit(solution)/shard_map/reshape | solution.py:513
  (30 shorter events, 0.2 us)
Async XLA Ops:
  10.1 4.1 %copy-start.8 = (f32[64,2,2048]{2,1,0:T(2,128)S(1)}, f32[64,2,2048]{2,1,0:T(2,128)}, u32[]{:S(2)}) copy-start(f32[64,2,2048]{2,1,0:T(2,128)} %param.7) | copy-start | bytes 3145732
  10.1 4.8 %copy-start.7 = (f32[4,2048]{1,0:T(4,128)S(1)}, f32[4,2048]{1,0:T(4,128)}, u32[]{:S(2)}) copy-start(f32[4,2048]{1,0:T(4,128)} %gain_ref.11) | copy-start | bytes 98308
  11.4 7.0 %copy-start.9 = (s32[4,2,1024]{2,1,0:T(2,128)S(1)}, s32[4,2,1024]{2,1,0:T(2,128)}, u32[]{:S(2)}) copy-start(s32[4,2,1024]{2,1,0:T(2,128)} %param.9) | copy-start | bytes 98308
  11.4 7.0 %copy-start.11 = (f32[4,4]{1,0:T(4,128)S(1)}, f32[4,4]{1,0:T(4,128)}, u32[]{:S(2)}) copy-start(f32[4,4]{1,0:T(4,128)} %param.10) | copy-start | bytes 196
  11.4 7.5 %copy-start.10 = (f32[4,2,1024]{2,1,0:T(2,128)S(1)}, f32[4,2,1024]{2,1,0:T(2,128)}, u32[]{:S(2)}) copy-start(f32[4,2,1024]{2,1,0:T(2,128)} %param.8) | copy-start | bytes 98308
  11.5 7.8 %copy-start.13 = (f32[8]{0:T(128)S(1)}, f32[8]{0:T(128)}, u32[]{:S(2)}) copy-start(f32[8]{0:T(128)} %constant.32.clone.1) | copy-start | bytes 100
  17.3 1.0 copy-start.3
  19.4 2.2 %copy-start = (bf16[32,128,512]{2,1,0:T(8,128)(2,1)S(1)}, bf16[32,128,512]{2,1,0:T(8,128)(2,1)}, u32[]{:S(2)}) copy-start(bf16[32,128,512]{2,1,0:T(8,128)(2,1)} %maximum_maximum_fusion) | copy-start | bytes 12582916
  41.6 4.9 %copy-start.12 = (f32[8]{0:T(128)S(1)}, f32[8]{0:T(128)}, u32[]{:S(2)}) copy-start(f32[8]{0:T(128)} %constant.31.clone.1) | copy-start | bytes 100
  41.6 5.0 %copy-start.1 = (bf16[32,128,512]{2,1,0:T(8,128)(2,1)S(1)}, bf16[32,128,512]{2,1,0:T(8,128)(2,1)}, u32[]{:S(2)}) copy-start(bf16[32,128,512]{2,1,0:T(8,128)(2,1)} %maximum_maximum_fusion) | copy-start | bytes 12582916
  68.5 1.0 copy-start.5
  70.2 2.2 %copy-start.2 = (bf16[32,128,512]{2,1,0:T(8,128)(2,1)S(1)}, bf16[32,128,512]{2,1,0:T(8,128)(2,1)}, u32[]{:S(2)}) copy-start(bf16[32,128,512]{2,1,0:T(8,128)(2,1)} %maximum_maximum_fusion) | copy-start | bytes 12582916
  72.4 22.7 %copy-start.4 = (f32[2,64,2048]{2,1,0:T(8,128)S(1)}, f32[2,64,2048]{2,1,0:T(8,128)}, u32[]{:S(2)}) copy-start(f32[2,64,2048]{2,1,0:T(8,128)} %copy-done.3) | copy-start | bytes 3145732
  72.4 22.7 %copy-start.6 = (f32[128,2048]{1,0:T(8,128)S(1)}, f32[128,2048]{1,0:T(8,128)}, u32[]{:S(2)}) copy-start(f32[128,2048]{1,0:T(8,128)} %copy-done.5) | copy-start | bytes 3145732

commit v2 on v1

--- a/solution.py
+++ b/solution.py
@@ -67,23 +67,34 @@
     )(messages)
 
 
+def peers(blk_count, quarter_count, act):
+    blk = lax.axis_index("blk")
+    quarter = lax.axis_index("quarter")
+    quarters = [lax.rem(quarter + i, quarter_count) for i in range(quarter_count)]
+    for other in quarters[1:]:
+        act(blk, other)
+
+    def visit(i, carry):
+        other_blk = lax.rem(blk + i, blk_count)
+        for other in quarters:
+            act(other_blk, other)
+        return carry
+
+    lax.fori_loop(1, blk_count, visit, 0)
+
+
 def scatter(me, blk_count, quarter_count, send_ref, per_blk, recv_ref, send_sem, recv_sem):
-    total = blk_count * quarter_count
-
-    def send(i, carry):
-        peer = lax.rem(me + i, total)
-        peer_blk = lax.div(peer, quarter_count)
+    def send(peer_blk, peer_quarter):
         pltpu.make_async_remote_copy(
-            src_ref=send_ref.at[peer_blk if per_blk else peer],
+            src_ref=send_ref.at[peer_blk if per_blk else peer_blk * quarter_count + peer_quarter],
             dst_ref=recv_ref.at[me],
             send_sem=send_sem,
             recv_sem=recv_sem,
-            device_id=(peer_blk, lax.rem(peer, quarter_count)),
+            device_id=(peer_blk, peer_quarter),
             device_id_type=MESH,
         ).start()
-        return carry
-
-    lax.fori_loop(1, total, send, 0)
+
+    peers(blk_count, quarter_count, send)
 
 
 def grid_kernel(
@@ -113,17 +124,12 @@
     me = blk * quarter_count + quarter
     barrier = pltpu.get_barrier_semaphore()
 
-    def greet(i, carry):
-        peer = lax.rem(me + i, total)
+    def greet(peer_blk, peer_quarter):
         pl.semaphore_signal(
-            barrier,
-            inc=1,
-            device_id=(lax.div(peer, quarter_count), lax.rem(peer, quarter_count)),
-            device_id_type=MESH,
-        )
-        return carry
-
-    lax.fori_loop(1, total, greet, 0)
+            barrier, inc=1, device_id=(peer_blk, peer_quarter), device_id_type=MESH
+        )
+
+    peers(blk_count, quarter_count, greet)
     arrived_ref[me] = send_ref[blk]
     pl.semaphore_wait(barrier, total - 1)
     scatter(me, blk_count, quarter_count, send_ref, True, arrived_ref, send_sem.at[0], recv_sem.at[0])
@@ -205,7 +211,7 @@
             pltpu.SemaphoreType.DMA((2,)),
         ],
         compiler_params=pltpu.CompilerParams(
-            collective_id=2, has_side_effects=True, vmem_limit_bytes=24 << 20
+            collective_id=2, has_side_effects=True, vmem_limit_bytes=14 << 20
         ),
         name="grid_stage",
     )(params, messages, old, weight, cos_rot, sin_rot, table)
@@ -260,7 +266,7 @@
             pltpu.VMEM((2 * lanes, degree_count), jnp.bfloat16),
             pltpu.VMEM((blk_count, rows, lanes), jnp.float32),
         ],
-        compiler_params=pltpu.CompilerParams(vmem_limit_bytes=24 << 20),
+        compiler_params=pltpu.CompilerParams(vmem_limit_bytes=14 << 20),
         name="synth_stage",
     )(values, factor, gains, sign, legendre_rows)
 
@@ -316,7 +322,7 @@
         in_specs=[pl.BlockSpec(memory_space=pltpu.VMEM)] * 4,
         out_specs=pl.BlockSpec(memory_space=pltpu.VMEM),
         scratch_shapes=[pltpu.VMEM((rows * lanes, legendre_rows.shape[0]), jnp.bfloat16)],
-        compiler_params=pltpu.CompilerParams(vmem_limit_bytes=24 << 20),
+        compiler_params=pltpu.CompilerParams(vmem_limit_bytes=14 << 20),
         name="adjoint_stage",
     )(returned, gains, sign, legendre_rows)
 
@@ -328,6 +334,41 @@
     for coef in (1.60217136e-04, -4.68162024e-03, 7.96925873e-02, -6.45964093e-01, 1.57079633):
         acc = acc * y + jnp.float32(coef)
     return acc * z
+
+
+def table_kernel(total, order_ref, table_ref):
+    rows, half_lon = table_ref.shape
+    slot_count = rows // total // 2
+    period = 4 * half_lon * lax.axis_size("quarter")
+    lane = lax.broadcasted_iota(jnp.int32, (slot_count, 128), 1)
+
+    def fill(d, carry):
+        orders = order_ref[pl.ds(pl.multiple_of(d * slot_count, slot_count), slot_count), :]
+        cos_b, sin_b = cos_sin(orders * (2 * lane + 1), period)
+        cos_a, sin_a = cos_sin(orders * (256 * lane), period)
+        at = pl.multiple_of(d * 2 * slot_count, 2 * slot_count)
+        for i in range(half_lon // 128):
+            cos_i, sin_i = cos_a[:, i : i + 1], sin_a[:, i : i + 1]
+            lon = slice(i * 128, (i + 1) * 128)
+            cosine = cos_i * cos_b - sin_i * sin_b
+            sine = sin_i * cos_b + cos_i * sin_b
+            table_ref[pl.ds(at, 2 * slot_count), lon] = jnp.concatenate([cosine, sine], 0).astype(
+                jnp.bfloat16
+            )
+        return carry
+
+    lax.fori_loop(0, total, fill, 0)
+
+
+def table_stage(orders, total, half_lon):
+    return pl.pallas_call(
+        functools.partial(table_kernel, total),
+        out_shape=jax.ShapeDtypeStruct((2 * orders.shape[0], half_lon), jnp.bfloat16),
+        in_specs=[pl.BlockSpec(memory_space=pltpu.VMEM)],
+        out_specs=pl.BlockSpec(memory_space=pltpu.VMEM),
+        compiler_params=pltpu.CompilerParams(vmem_limit_bytes=14 << 20),
+        name="table_stage",
+    )(orders)
 
 
 def cos_sin(steps, period):
@@ -370,35 +411,30 @@
     first_slot = (blk_index * quarter_count + quarter_index) * slot_count
     my_orders = lax.dynamic_slice_in_dim(order_table, first_slot, slot_count)
 
-    tile = min(128, half_lon)
-    coarse = jnp.arange(half_lon // tile, dtype=jnp.int32) * tile
-    fine = 2 * jnp.arange(tile, dtype=jnp.int32) + 1
-    cos_a, sin_a = cos_sin(order_table[:, None] * (2 * coarse)[None, :], 2 * lon_total)
-    cos_b, sin_b = cos_sin(order_table[:, None] * fine[None, :], 2 * lon_total)
+    fused = lanes == 128 and rows == 8 and cycle_local == 2 and cycle_pairs == blk_count and half_lon % 128 == 0
     centre = 2 * lon_local * quarter_index + (lon_local - 1)
     cos_c, sin_c = cos_sin(order_table * centre, 2 * lon_total)
-    cos_a, sin_a, cos_b, sin_b, cos_c, sin_c = lax.optimization_barrier(
-        (cos_a, sin_a, cos_b, sin_b, cos_c, sin_c)
-    )
-    cos_table = jnp.concatenate(
-        [cos_a[:, i : i + 1] * cos_b - sin_a[:, i : i + 1] * sin_b for i in range(coarse.shape[0])], 1
-    ).astype(bf16)
-    sin_table = jnp.concatenate(
-        [sin_a[:, i : i + 1] * cos_b + cos_a[:, i : i + 1] * sin_b for i in range(coarse.shape[0])], 1
-    ).astype(bf16)
-    fused = lanes == 128 and rows == 8 and cycle_local == 2 and cycle_pairs == blk_count
     if fused:
-        table = jnp.concatenate(
-            [
-                cos_table.reshape(total, slot_count, half_lon),
-                sin_table.reshape(total, slot_count, half_lon),
-            ],
-            1,
-        ).reshape(total * lanes, half_lon)
+        table = table_stage(order_table[:, None], total, half_lon)
         cos_c = cos_c.reshape(total, 1, slot_count)
         sin_c = sin_c.reshape(total, 1, slot_count)
         cos_rot = jnp.concatenate([cos_c, cos_c], 2)
         sin_rot = jnp.concatenate([sin_c, -sin_c], 2)
+    else:
+        tile = min(128, half_lon)
+        coarse = jnp.arange(half_lon // tile, dtype=jnp.int32) * tile
+        fine = 2 * jnp.arange(tile, dtype=jnp.int32) + 1
+        cos_a, sin_a = cos_sin(order_table[:, None] * (2 * coarse)[None, :], 2 * lon_total)
+        cos_b, sin_b = cos_sin(order_table[:, None] * fine[None, :], 2 * lon_total)
+        cos_a, sin_a, cos_b, sin_b, cos_c, sin_c = lax.optimization_barrier(
+            (cos_a, sin_a, cos_b, sin_b, cos_c, sin_c)
+        )
+        cos_table = jnp.concatenate(
+            [cos_a[:, i : i + 1] * cos_b - sin_a[:, i : i + 1] * sin_b for i in range(coarse.shape[0])], 1
+        ).astype(bf16)
+        sin_table = jnp.concatenate(
+            [sin_a[:, i : i + 1] * cos_b + cos_a[:, i : i + 1] * sin_b for i in range(coarse.shape[0])], 1
+        ).astype(bf16)
 
     pair_index = blk_index * (cycle_local // 2) + jnp.arange(cycle_local // 2, dtype=jnp.int32)
     theta = (pair_index.astype(jnp.float32) + 0.5) * (math.pi / (2 * cycle_pairs))

time: 99.6 us -> 96 us (0.964)
  other arithmetic: 11.2 us -> 1.86 us
  Pallas kernels: 66.4 us -> 74.3 us
  local copies, waits for them, and re-layouts: 16.4 us -> 14.7 us
    pallas_call x0 -> x1, Pallas kernels: none -> 7.56 us  [table_stage(): pl.pallas_call(functools.partial(table_kernel, total), out_shape=jax.Shap...]
    mul x3 -> x1, other arithmetic: 3.78 us -> 0.02 us  [half_turn_sine(): return acc * z]
    another operation x1 -> x0, other arithmetic: 2.84 us -> none
    concatenate x1 -> x0, other arithmetic: 2.79 us -> none  [body(): jnp.concatenate([cos_table.reshape(total, slot_count, half_lon), sin_tabl...]
    unnamed x28, local copies, waits for them, and re-layouts: 6.36 us -> 4.24 us
where the time goes in v2:
time: 96 us; the launch traced here: 95.7 us
  Pallas kernels  74.3 us (77%)
  local copies, waits for them, and re-layouts  14.7 us (15%)
  between operations  4.85 us (5%)
  other arithmetic  1.86 us (2%)
    pallas_call x3, Pallas kernels, grid_stage(): pl.pallas_call(functools.partial(grid_kernel, blk_count, quarter_count, s...  52.1 us
    pallas_call x1, Pallas kernels, table_stage(): pl.pallas_call(functools.partial(table_kernel, total), out_shape=jax.Shap...  7.56 us
    pallas_call x3, Pallas kernels, synth_stage(): pl.pallas_call(functools.partial(synth_kernel, blk_count), out_shape=jax....  7.31 us
    pallas_call x3, Pallas kernels, adjoint_stage(): pl.pallas_call(functools.partial(adjoint_kernel, blk_count), out_shape=ja...  7.29 us
    unnamed x28, local copies, waits for them, and re-layouts  4.24 us
    reshape x2, local copies, waits for them, and re-layouts, body(): out.reshape(2, slot_count, degree_count).transpose(1, 0, 2)  3.56 us
    transpose x1, local copies, waits for them, and re-layouts, body(): legendre.transpose(1, 0, 2).reshape(cycle_pairs * slot_count, degree_count)  2.83 us

profile of v2, /device:TPU:0, one launch (start us, length us, event | category | flops | bytes accessed | tf_op | source)
XLA Modules:
  0.0 95.7 jit_solution(5874778218758912114)
XLA Ops:
  0.6 0.8 fusion.8
  1.4 0.1 maximum_bitcast_fusion
  1.5 0.1 copy.32.sign_ref
  1.6 2.8 %copy.31 = bf16[8,64,2048]{2,1,0:T(8,128)(2,1)S(1)} copy(bf16[8,64,2048]{2,0,1:T(8,128)(2,1)} %bitcast.31) | data formatting | bytes 4194304 | tf_op jit(solution)/shard_map/transpose | solution.py:516
  4.4 0.0 copy-start.6
  4.5 0.6 copy.30
  5.1 0.0 copy-start.8
  5.1 0.0 copy-start.9
  5.1 0.0 copy-start.11
  5.1 0.0 copy-start.10
  5.1 0.1 copy-done.6
  5.2 2.4 %synth_stage.3.send_ref = bf16[8,16,128]{2,1,0:T(8,128)(2,1)S(1)} custom-call(f32[128,2048]{1,0:T(8,128)S(1)} %bitcast.28, f32[1,2048]{1,0:T(1,128)S(1)} %broadcast_in_dim.46.factor_ref, f32[4,2048]{1,0:T(4,128)S(1)} %copy-done.6, f32[128,1]{1,0:T(8,128)S(1)} %copy.32.sign_ref, bf16[512,2048]{1,0:T(8,128)(2,1)S(1)} %bitcast.22), custom_call_target="tpu_custom_call" | custom-call | tf_op jit(solution)/shard_map/synth_stage/pallas_call | solution.py:260
  7.6 0.0 copy-start.2
  7.6 1.0 %copy-done.2 = f32[2,64,2048]{2,1,0:T(8,128)} copy-done((f32[2,64,2048]{2,1,0:T(8,128)}, f32[2,64,2048]{2,1,0:T(8,128)S(1)}, u32[]{:S(2)}) %copy-start.2) | copy-done | bytes 1048600
  8.6 0.1 reshape.78
  8.7 0.1 reshape.77
  8.8 0.1 pad_maximum_fusion.2
  9.1 0.2 select_reduce_fusion
  9.3 0.5 rev.8
  9.8 0.3 rev.7
  10.1 0.4 copy.33.order_ref
  10.5 0.0 copy-start.13
  10.5 7.6 %table_stage.1.table_ref = bf16[4096,512]{1,0:T(8,128)(2,1)S(1)} custom-call(s32[2048,1]{1,0:T(8,128)S(1)} %copy.33.order_ref), custom_call_target="tpu_custom_call" | custom-call | tf_op jit(solution)/shard_map/table_stage/pallas_call | solution.py:364
  18.1 0.1 broadcast_in_dim.45.params_ref
  18.2 20.2 %grid_stage.3 = (f32[8,8,128]{2,1,0:T(8,128)S(1)}, f32[16,512]{1,0:T(8,128)}, f32[8,128]{1,0:T(8,128)}) custom-call(f32[8,128]{1,0:T(8,128)S(1)} %broadcast_in_dim.45.params_ref, bf16[8,16,128]{2,1,0:T(8,128)(2,1)S(1)} %synth_stage.3.send_ref, f32[16,512]{1,0:T(8,128)S(1)} %get-tuple-element.26.old_ref, f32[16,512]{1,0:T(8,128)S(1)} %get-tuple-element.27.weight_ref, ...), custom_call_target="tpu_custom_call" | custom-call | tf_op jit(solution)/shard_map/grid_stage/pallas_call | solution.py:196
  38.4 2.4 %adjoint_stage.3.values_ref = f32[128,2048]{1,0:T(8,128)S(1)} custom-call(f32[8,8,128]{2,1,0:T(8,128)S(1)} %get-tuple-element.8.returned_ref, f32[4,2048]{1,0:T(4,128)S(1)} %copy-done.6, f32[128,1]{1,0:T(8,128)S(1)} %copy.32.sign_ref, bf16[512,2048]{1,0:T(8,128)(2,1)S(1)} %bitcast.23), custom_call_target="tpu_custom_call" | custom-call | tf_op jit(solution)/shard_map/adjoint_stage/pallas_call | solution.py:319
  40.8 0.0 copy-start.12
  40.8 2.4 %synth_stage.4.send_ref = bf16[8,16,128]{2,1,0:T(8,128)(2,1)S(1)} custom-call(f32[128,2048]{1,0:T(8,128)S(1)} %adjoint_stage.3.values_ref, f32[1,2048]{1,0:T(1,128)S(1)} %add_divide_fusion.1.factor_ref, f32[4,2048]{1,0:T(4,128)S(1)} %copy-done.6, f32[128,1]{1,0:T(8,128)S(1)} %copy.32.sign_ref, bf16[512,2048]{1,0:T(8,128)(2,1)S(1)} %bitcast.24), custom_call_target="tpu_custom_call" | custom-call | tf_op jit(solution)/shard_map/synth_stage/pallas_call | solution.py:260
  43.3 0.0 copy-done.12
  43.3 0.1 broadcast_in_dim.44.params_ref
  43.3 15.0 %grid_stage.4 = (f32[8,8,128]{2,1,0:T(8,128)S(1)}, f32[16,512]{1,0:T(8,128)S(1)}, f32[8,128]{1,0:T(8,128)S(1)}) custom-call(f32[8,128]{1,0:T(8,128)S(1)} %broadcast_in_dim.44.params_ref, bf16[8,16,128]{2,1,0:T(8,128)(2,1)S(1)} %synth_stage.4.send_ref, f32[16,512]{1,0:T(8,128)S(1)} %get-tuple-element.26.old_ref, f32[16,512]{1,0:T(8,128)S(1)} %get-tuple-element.27.weight_ref, ...), custom_call_target="tpu_custom_call" | custom-call | tf_op jit(solution)/shard_map/grid_stage/pallas_call | solution.py:196
  58.3 0.5 fusion.13
  60.1 2.4 %adjoint_stage.4 = f32[128,2048]{1,0:T(8,128)S(1)} custom-call(f32[8,8,128]{2,1,0:T(8,128)S(1)} %get-tuple-element.10.returned_ref, f32[4,2048]{1,0:T(4,128)S(1)} %copy-done.6, f32[128,1]{1,0:T(8,128)S(1)} %copy.32.sign_ref, bf16[512,2048]{1,0:T(8,128)(2,1)S(1)} %bitcast.25), custom_call_target="tpu_custom_call" | custom-call | tf_op jit(solution)/shard_map/adjoint_stage/pallas_call | solution.py:319
  62.5 0.1 multiply_subtract_fusion.1.values_ref
  62.7 2.5 %synth_stage.5.send_ref = bf16[8,16,128]{2,1,0:T(8,128)(2,1)S(1)} custom-call(f32[128,2048]{1,0:T(8,128)S(1)} %multiply_subtract_fusion.1.values_ref, f32[1,2048]{1,0:T(1,128)S(1)} %add_divide_fusion.1.factor_ref, f32[4,2048]{1,0:T(4,128)S(1)} %copy-done.6, f32[128,1]{1,0:T(8,128)S(1)} %copy.32.sign_ref, bf16[512,2048]{1,0:T(8,128)(2,1)S(1)} %bitcast.26), custom_call_target="tpu_custom_call" | custom-call | tf_op jit(solution)/shard_map/synth_stage/pallas_call | solution.py:260
  65.1 0.0 copy-start.4
  65.2 1.0 %copy-done.4 = f32[128,2048]{1,0:T(8,128)} copy-done((f32[128,2048]{1,0:T(8,128)}, f32[128,2048]{1,0:T(8,128)S(1)}, u32[]{:S(2)}) %copy-start.4) | copy-done | bytes 1048600
  66.1 0.6 stack.3
  66.8 0.1 broadcast_in_dim.52.params_ref
  66.8 2.2 %copy-done.1 = bf16[4096,512]{1,0:T(8,128)(2,1)S(1)} copy-done((bf16[4096,512]{1,0:T(8,128)(2,1)S(1)}, bf16[4096,512]{1,0:T(8,128)(2,1)}, u32[]{:S(2)}) %copy-start.1) | copy-done | bytes 4194328
  69.0 17.0 %grid_stage.5 = (f32[8,8,128]{2,1,0:T(8,128)S(1)}, f32[16,512]{1,0:T(8,128)}, f32[8,128]{1,0:T(8,128)S(1)}) custom-call(f32[8,128]{1,0:T(8,128)S(1)} %broadcast_in_dim.52.params_ref, bf16[8,16,128]{2,1,0:T(8,128)(2,1)S(1)} %synth_stage.5.send_ref, f32[16,512]{1,0:T(8,128)S(1)} %get-tuple-element.11.old_ref, f32[16,512]{1,0:T(8,128)S(1)} %get-tuple-element.27.weight_ref, ...), custom_call_target="tpu_custom_call" | custom-call | tf_op jit(solution)/shard_map/grid_stage/pallas_call | solution.py:196
  86.0 0.0 copy-start.3
  86.0 0.0 copy-start.5
  86.1 0.6 fusion.12
  89.2 2.4 %adjoint_stage.5 = f32[128,2048]{1,0:T(8,128)S(1)} custom-call(f32[8,8,128]{2,1,0:T(8,128)S(1)} %get-tuple-element.13.returned_ref, f32[4,2048]{1,0:T(4,128)S(1)} %copy-done.6, f32[128,1]{1,0:T(8,128)S(1)} %copy.32.sign_ref, bf16[512,2048]{1,0:T(8,128)(2,1)S(1)} %bitcast.27), custom_call_target="tpu_custom_call" | custom-call | tf_op jit(solution)/shard_map/adjoint_stage/pallas_call | solution.py:319
  91.7 0.5 multiply_subtract_fusion
  92.2 1.8 %copy.43 = f32[2,64,2048]{2,0,1:T(2,128)} copy(f32[2,64,2048]{2,1,0:T(8,128)S(1)} %bitcast.30) | data formatting | bytes 2097152 | tf_op jit(solution)/shard_map/reshape | solution.py:549
  93.9 1.8 %copy.44 = f32[2,64,2048]{2,0,1:T(2,128)} copy(f32[2,64,2048]{2,1,0:T(8,128)S(1)} %bitcast.29) | data formatting | bytes 2097152 | tf_op jit(solution)/shard_map/reshape | solution.py:549
  (25 shorter events, 0.2 us)
Async XLA Ops:
  1.6 2.9 %copy-start.7 = (f32[64,2,2048]{2,1,0:T(2,128)S(1)}, f32[64,2,2048]{2,1,0:T(2,128)}, u32[]{:S(2)}) copy-start(f32[64,2,2048]{2,1,0:T(2,128)} %param.7) | copy-start | bytes 3145732
  4.4 0.8 copy-start.6
  5.1 3.5 %copy-start.8 = (s32[2048]{0:T(1024)S(1)}, s32[2048]{0:T(1024)}, u32[]{:S(2)}) copy-start(s32[2048]{0:T(1024)} %param.13) | copy-start | bytes 24580
  5.1 4.0 %copy-start.9 = (s32[4,2,1024]{2,1,0:T(2,128)S(1)}, s32[4,2,1024]{2,1,0:T(2,128)}, u32[]{:S(2)}) copy-start(s32[4,2,1024]{2,1,0:T(2,128)} %param.9) | copy-start | bytes 98308
  5.1 4.0 %copy-start.11 = (f32[4,4]{1,0:T(4,128)S(1)}, f32[4,4]{1,0:T(4,128)}, u32[]{:S(2)}) copy-start(f32[4,4]{1,0:T(4,128)} %param.10) | copy-start | bytes 196
  5.1 4.7 %copy-start.10 = (f32[4,2,1024]{2,1,0:T(2,128)S(1)}, f32[4,2,1024]{2,1,0:T(2,128)}, u32[]{:S(2)}) copy-start(f32[4,2,1024]{2,1,0:T(2,128)} %param.8) | copy-start | bytes 98308
  7.6 1.0 %copy-start.2 = (f32[2,64,2048]{2,1,0:T(8,128)}, f32[2,64,2048]{2,1,0:T(8,128)S(1)}, u32[]{:S(2)}) copy-start(f32[2,64,2048]{2,1,0:T(8,128)S(1)} %copy.30) | copy-start | bytes 3145732
  10.5 7.6 %copy-start.13 = (f32[8]{0:T(128)S(1)}, f32[8]{0:T(128)}, u32[]{:S(2)}) copy-start(f32[8]{0:T(128)} %constant.29.clone.1) | copy-start | bytes 100
  18.1 25.2 %copy-start = (bf16[4096,512]{1,0:T(8,128)(2,1)}, bf16[4096,512]{1,0:T(8,128)(2,1)S(1)}, u32[]{:S(2)}) copy-start(bf16[4096,512]{1,0:T(8,128)(2,1)S(1)} %table_stage.1.table_ref) | copy-start | bytes 12582916
  40.8 2.5 %copy-start.12 = (f32[8]{0:T(128)S(1)}, f32[8]{0:T(128)}, u32[]{:S(2)}) copy-start(f32[8]{0:T(128)} %constant.28.clone.1) | copy-start | bytes 100
  65.1 1.0 %copy-start.4 = (f32[128,2048]{1,0:T(8,128)}, f32[128,2048]{1,0:T(8,128)S(1)}, u32[]{:S(2)}) copy-start(f32[128,2048]{1,0:T(8,128)S(1)} %multiply_subtract_fusion.1.values_ref) | copy-start | bytes 3145732
  66.8 2.2 %copy-start.1 = (bf16[4096,512]{1,0:T(8,128)(2,1)S(1)}, bf16[4096,512]{1,0:T(8,128)(2,1)}, u32[]{:S(2)}) copy-start(bf16[4096,512]{1,0:T(8,128)(2,1)} %copy-done) | copy-start | bytes 12582916
  86.0 5.6 %copy-start.3 = (f32[2,64,2048]{2,1,0:T(8,128)S(1)}, f32[2,64,2048]{2,1,0:T(8,128)}, u32[]{:S(2)}) copy-start(f32[2,64,2048]{2,1,0:T(8,128)} %copy-done.2) | copy-start | bytes 3145732
  86.0 5.6 %copy-start.5 = (f32[128,2048]{1,0:T(8,128)S(1)}, f32[128,2048]{1,0:T(8,128)}, u32[]{:S(2)}) copy-start(f32[128,2048]{1,0:T(8,128)} %copy-done.4) | copy-start | bytes 3145732

commit v3 on v2

--- a/solution.py
+++ b/solution.py
@@ -83,10 +83,10 @@
     lax.fori_loop(1, blk_count, visit, 0)
 
 
-def scatter(me, blk_count, quarter_count, send_ref, per_blk, recv_ref, send_sem, recv_sem):
+def scatter(me, blk_count, quarter_count, send_ref, recv_ref, send_sem, recv_sem):
     def send(peer_blk, peer_quarter):
         pltpu.make_async_remote_copy(
-            src_ref=send_ref.at[peer_blk if per_blk else peer_blk * quarter_count + peer_quarter],
+            src_ref=send_ref.at[peer_blk],
             dst_ref=recv_ref.at[me],
             send_sem=send_sem,
             recv_sem=recv_sem,
@@ -132,7 +132,7 @@
     peers(blk_count, quarter_count, greet)
     arrived_ref[me] = send_ref[blk]
     pl.semaphore_wait(barrier, total - 1)
-    scatter(me, blk_count, quarter_count, send_ref, True, arrived_ref, send_sem.at[0], recv_sem.at[0])
+    scatter(me, blk_count, quarter_count, send_ref, arrived_ref, send_sem.at[0], recv_sem.at[0])
     some = arrived_ref.at[pl.ds(0, total - 1)]
     pltpu.make_async_copy(some, some, recv_sem.at[0]).wait()
 
@@ -164,18 +164,34 @@
     tail = jnp.where(row == 0, high, jnp.where(row == 1, middle, jnp.where(row == 2, low, 0.0)))
     plus, minus = weighted[:rows], weighted[rows:]
     folded = jnp.concatenate([plus + minus, plus - minus], 0).astype(jnp.bfloat16)
-    back = lax.dot_general(
-        folded, table_ref[...], (((1,), (1,)), ((), ())), preferred_element_type=jnp.float32
-    )
     cos_lanes = lax.broadcasted_iota(jnp.int32, (rows, lanes), 1) < lanes // 2
-    for d in range(total):
-        part = back[:, d * lanes : (d + 1) * lanes]
-        picked = scale * jnp.where(cos_lanes, part[:rows], part[rows:])
-        share = picked * cos_ref[d] - pltpu.roll(picked, lanes // 2, 1) * sin_ref[d]
-        shares_ref[d] = jnp.concatenate([share, tail], 0).astype(jnp.bfloat16)
+    width = quarter_count * lanes
+    quarters = [lax.rem(quarter + i, quarter_count) for i in range(quarter_count)]
+    for i in range(1, blk_count + 1):
+        chunk = lax.rem(blk + i, blk_count)
+        back = lax.dot_general(
+            folded,
+            table_ref[pl.ds(pl.multiple_of(chunk * width, width), width), :],
+            (((1,), (1,)), ((), ())),
+            preferred_element_type=jnp.float32,
+        )
+        for q in range(quarter_count):
+            d = chunk * quarter_count + q
+            part = back[:, q * lanes : (q + 1) * lanes]
+            picked = scale * jnp.where(cos_lanes, part[:rows], part[rows:])
+            share = picked * cos_ref[d] - pltpu.roll(picked, lanes // 2, 1) * sin_ref[d]
+            shares_ref[d] = jnp.concatenate([share, tail], 0).astype(jnp.bfloat16)
+        for other in quarters[1:] if i == blk_count else quarters:
+            pltpu.make_async_remote_copy(
+                src_ref=shares_ref.at[chunk * quarter_count + other],
+                dst_ref=landed_ref.at[me],
+                send_sem=send_sem.at[1],
+                recv_sem=recv_sem.at[1],
+                device_id=(chunk, other),
+                device_id_type=MESH,
+            ).start()
 
     landed_ref[me] = shares_ref[me]
-    scatter(me, blk_count, quarter_count, shares_ref, False, landed_ref, send_sem.at[1], recv_sem.at[1])
     some = landed_ref.at[pl.ds(0, total - 1)]
     pltpu.make_async_copy(some, some, recv_sem.at[1]).wait()
     landed = landed_ref[...].astype(jnp.float32)
@@ -341,11 +357,14 @@
     slot_count = rows // total // 2
     period = 4 * half_lon * lax.axis_size("quarter")
     lane = lax.broadcasted_iota(jnp.int32, (slot_count, 128), 1)
+    fine = (2 * lane + 1).astype(jnp.float32)
+    coarse = (256 * jnp.minimum(lane, half_lon // 128)).astype(jnp.float32)
 
     def fill(d, carry):
         orders = order_ref[pl.ds(pl.multiple_of(d * slot_count, slot_count), slot_count), :]
-        cos_b, sin_b = cos_sin(orders * (2 * lane + 1), period)
-        cos_a, sin_a = cos_sin(orders * (256 * lane), period)
+        orders = orders.astype(jnp.float32)
+        cos_b, sin_b = cos_sin((orders * fine).astype(jnp.int32), period)
+        cos_a, sin_a = cos_sin((orders * coarse).astype(jnp.int32), period)
         at = pl.multiple_of(d * 2 * slot_count, 2 * slot_count)
         for i in range(half_lon // 128):
             cos_i, sin_i = cos_a[:, i : i + 1], sin_a[:, i : i + 1]
@@ -357,7 +376,7 @@
             )
         return carry
 
-    lax.fori_loop(0, total, fill, 0)
+    lax.fori_loop(0, total, fill, 0, unroll=2)
 
 
 def table_stage(orders, total, half_lon):

time: 96 us -> 92.7 us (0.966)
  Pallas kernels: 74.3 us -> 70.9 us
    pallas_call x1, Pallas kernels: 7.56 us -> 5.59 us  [table_stage(): pl.pallas_call(functools.partial(table_kernel, total), out_shape=jax.Shap...]
    pallas_call x3, Pallas kernels: 52.1 us -> 50.7 us  [grid_stage(): pl.pallas_call(functools.partial(grid_kernel, blk_count, quarter_count, s...]
where the time goes in v3:
time: 92.7 us; the launch traced here: 92.3 us
  Pallas kernels  70.9 us (76%)
  local copies, waits for them, and re-layouts  14.7 us (16%)
  between operations  4.85 us (5%)
  other arithmetic  1.86 us (2%)
    pallas_call x3, Pallas kernels, grid_stage(): pl.pallas_call(functools.partial(grid_kernel, blk_count, quarter_count, s...  50.7 us
    pallas_call x3, Pallas kernels, synth_stage(): pl.pallas_call(functools.partial(synth_kernel, blk_count), out_shape=jax....  7.31 us
    pallas_call x3, Pallas kernels, adjoint_stage(): pl.pallas_call(functools.partial(adjoint_kernel, blk_count), out_shape=ja...  7.3 us
    pallas_call x1, Pallas kernels, table_stage(): pl.pallas_call(functools.partial(table_kernel, total), out_shape=jax.Shap...  5.59 us
    unnamed x28, local copies, waits for them, and re-layouts  4.24 us
    reshape x2, local copies, waits for them, and re-layouts, body(): out.reshape(2, slot_count, degree_count).transpose(1, 0, 2)  3.56 us
    transpose x1, local copies, waits for them, and re-layouts, body(): legendre.transpose(1, 0, 2).reshape(cycle_pairs * slot_count, degree_count)  2.83 us

profile of v3, /device:TPU:0, one launch (start us, length us, event | category | flops | bytes accessed | tf_op | source)
XLA Modules:
  0.0 92.3 jit_solution(13598007436672092305)
XLA Ops:
  0.6 0.8 fusion.8
  1.4 0.1 maximum_bitcast_fusion
  1.5 0.1 copy.32.sign_ref
  1.6 2.8 %copy.31 = bf16[8,64,2048]{2,1,0:T(8,128)(2,1)S(1)} copy(bf16[8,64,2048]{2,0,1:T(8,128)(2,1)} %bitcast.31) | data formatting | bytes 4194304 | tf_op jit(solution)/shard_map/transpose | solution.py:535
  4.4 0.0 copy-start.6
  4.5 0.0 copy-done.7
  4.5 0.6 copy.30
  5.1 0.0 copy-start.8
  5.1 0.0 copy-start.9
  5.1 0.0 copy-start.11
  5.1 0.0 copy-start.10
  5.1 0.1 copy-done.6
  5.2 2.4 %synth_stage.3.send_ref = bf16[8,16,128]{2,1,0:T(8,128)(2,1)S(1)} custom-call(f32[128,2048]{1,0:T(8,128)S(1)} %bitcast.28, f32[1,2048]{1,0:T(1,128)S(1)} %broadcast_in_dim.46.factor_ref, f32[4,2048]{1,0:T(4,128)S(1)} %copy-done.6, f32[128,1]{1,0:T(8,128)S(1)} %copy.32.sign_ref, bf16[512,2048]{1,0:T(8,128)(2,1)S(1)} %bitcast.22), custom_call_target="tpu_custom_call" | custom-call | tf_op jit(solution)/shard_map/synth_stage/pallas_call | solution.py:276
  7.6 0.0 copy-start.2
  7.6 1.0 %copy-done.2 = f32[2,64,2048]{2,1,0:T(8,128)} copy-done((f32[2,64,2048]{2,1,0:T(8,128)}, f32[2,64,2048]{2,1,0:T(8,128)S(1)}, u32[]{:S(2)}) %copy-start.2) | copy-done | bytes 1048600
  8.6 0.1 reshape.78
  8.7 0.1 reshape.77
  8.8 0.1 pad_maximum_fusion.2
  9.1 0.2 select_reduce_fusion
  9.3 0.5 rev.8
  9.8 0.3 rev.7
  10.1 0.4 copy.33.order_ref
  10.5 0.0 copy-start.13
  10.5 5.6 %table_stage.1.table_ref = bf16[4096,512]{1,0:T(8,128)(2,1)S(1)} custom-call(s32[2048,1]{1,0:T(8,128)S(1)} %copy.33.order_ref), custom_call_target="tpu_custom_call" | custom-call | tf_op jit(solution)/shard_map/table_stage/pallas_call | solution.py:383
  16.2 0.1 broadcast_in_dim.45.params_ref
  16.2 19.3 %grid_stage.3 = (f32[8,8,128]{2,1,0:T(8,128)S(1)}, f32[16,512]{1,0:T(8,128)}, f32[8,128]{1,0:T(8,128)}) custom-call(f32[8,128]{1,0:T(8,128)S(1)} %broadcast_in_dim.45.params_ref, bf16[8,16,128]{2,1,0:T(8,128)(2,1)S(1)} %synth_stage.3.send_ref, f32[16,512]{1,0:T(8,128)S(1)} %get-tuple-element.26.old_ref, f32[16,512]{1,0:T(8,128)S(1)} %get-tuple-element.27.weight_ref, ...), custom_call_target="tpu_custom_call" | custom-call | tf_op jit(solution)/shard_map/grid_stage/pallas_call | solution.py:212
  35.5 2.4 %adjoint_stage.3.values_ref = f32[128,2048]{1,0:T(8,128)S(1)} custom-call(f32[8,8,128]{2,1,0:T(8,128)S(1)} %get-tuple-element.8.returned_ref, f32[4,2048]{1,0:T(4,128)S(1)} %copy-done.6, f32[128,1]{1,0:T(8,128)S(1)} %copy.32.sign_ref, bf16[512,2048]{1,0:T(8,128)(2,1)S(1)} %bitcast.23), custom_call_target="tpu_custom_call" | custom-call | tf_op jit(solution)/shard_map/adjoint_stage/pallas_call | solution.py:335
  37.9 0.0 copy-start.12
  38.0 2.4 %synth_stage.4.send_ref = bf16[8,16,128]{2,1,0:T(8,128)(2,1)S(1)} custom-call(f32[128,2048]{1,0:T(8,128)S(1)} %adjoint_stage.3.values_ref, f32[1,2048]{1,0:T(1,128)S(1)} %add_divide_fusion.1.factor_ref, f32[4,2048]{1,0:T(4,128)S(1)} %copy-done.6, f32[128,1]{1,0:T(8,128)S(1)} %copy.32.sign_ref, bf16[512,2048]{1,0:T(8,128)(2,1)S(1)} %bitcast.24), custom_call_target="tpu_custom_call" | custom-call | tf_op jit(solution)/shard_map/synth_stage/pallas_call | solution.py:276
  40.4 0.1 broadcast_in_dim.44.params_ref
  40.5 15.0 %grid_stage.4 = (f32[8,8,128]{2,1,0:T(8,128)S(1)}, f32[16,512]{1,0:T(8,128)S(1)}, f32[8,128]{1,0:T(8,128)S(1)}) custom-call(f32[8,128]{1,0:T(8,128)S(1)} %broadcast_in_dim.44.params_ref, bf16[8,16,128]{2,1,0:T(8,128)(2,1)S(1)} %synth_stage.4.send_ref, f32[16,512]{1,0:T(8,128)S(1)} %get-tuple-element.26.old_ref, f32[16,512]{1,0:T(8,128)S(1)} %get-tuple-element.27.weight_ref, ...), custom_call_target="tpu_custom_call" | custom-call | tf_op jit(solution)/shard_map/grid_stage/pallas_call | solution.py:212
  55.5 0.5 fusion.13
  57.2 2.4 %adjoint_stage.4 = f32[128,2048]{1,0:T(8,128)S(1)} custom-call(f32[8,8,128]{2,1,0:T(8,128)S(1)} %get-tuple-element.10.returned_ref, f32[4,2048]{1,0:T(4,128)S(1)} %copy-done.6, f32[128,1]{1,0:T(8,128)S(1)} %copy.32.sign_ref, bf16[512,2048]{1,0:T(8,128)(2,1)S(1)} %bitcast.25), custom_call_target="tpu_custom_call" | custom-call | tf_op jit(solution)/shard_map/adjoint_stage/pallas_call | solution.py:335
  59.7 0.1 multiply_subtract_fusion.1.values_ref
  59.8 2.5 %synth_stage.5.send_ref = bf16[8,16,128]{2,1,0:T(8,128)(2,1)S(1)} custom-call(f32[128,2048]{1,0:T(8,128)S(1)} %multiply_subtract_fusion.1.values_ref, f32[1,2048]{1,0:T(1,128)S(1)} %add_divide_fusion.1.factor_ref, f32[4,2048]{1,0:T(4,128)S(1)} %copy-done.6, f32[128,1]{1,0:T(8,128)S(1)} %copy.32.sign_ref, bf16[512,2048]{1,0:T(8,128)(2,1)S(1)} %bitcast.26), custom_call_target="tpu_custom_call" | custom-call | tf_op jit(solution)/shard_map/synth_stage/pallas_call | solution.py:276
  62.3 0.0 copy-start.4
  62.3 1.0 %copy-done.4 = f32[128,2048]{1,0:T(8,128)} copy-done((f32[128,2048]{1,0:T(8,128)}, f32[128,2048]{1,0:T(8,128)S(1)}, u32[]{:S(2)}) %copy-start.4) | copy-done | bytes 1048600
  63.3 0.6 stack.3
  63.9 0.1 broadcast_in_dim.52.params_ref
  64.0 2.2 %copy-done.1 = bf16[4096,512]{1,0:T(8,128)(2,1)S(1)} copy-done((bf16[4096,512]{1,0:T(8,128)(2,1)S(1)}, bf16[4096,512]{1,0:T(8,128)(2,1)}, u32[]{:S(2)}) %copy-start.1) | copy-done | bytes 4194328
  66.2 16.5 %grid_stage.5 = (f32[8,8,128]{2,1,0:T(8,128)S(1)}, f32[16,512]{1,0:T(8,128)}, f32[8,128]{1,0:T(8,128)S(1)}) custom-call(f32[8,128]{1,0:T(8,128)S(1)} %broadcast_in_dim.52.params_ref, bf16[8,16,128]{2,1,0:T(8,128)(2,1)S(1)} %synth_stage.5.send_ref, f32[16,512]{1,0:T(8,128)S(1)} %get-tuple-element.11.old_ref, f32[16,512]{1,0:T(8,128)S(1)} %get-tuple-element.27.weight_ref, ...), custom_call_target="tpu_custom_call" | custom-call | tf_op jit(solution)/shard_map/grid_stage/pallas_call | solution.py:212
  82.7 0.0 copy-start.3
  82.7 0.0 copy-start.5
  82.7 0.6 fusion.12
  85.8 2.4 %adjoint_stage.5 = f32[128,2048]{1,0:T(8,128)S(1)} custom-call(f32[8,8,128]{2,1,0:T(8,128)S(1)} %get-tuple-element.13.returned_ref, f32[4,2048]{1,0:T(4,128)S(1)} %copy-done.6, f32[128,1]{1,0:T(8,128)S(1)} %copy.32.sign_ref, bf16[512,2048]{1,0:T(8,128)(2,1)S(1)} %bitcast.27), custom_call_target="tpu_custom_call" | custom-call | tf_op jit(solution)/shard_map/adjoint_stage/pallas_call | solution.py:335
  88.3 0.5 multiply_subtract_fusion
  88.8 1.8 %copy.43 = f32[2,64,2048]{2,0,1:T(2,128)} copy(f32[2,64,2048]{2,1,0:T(8,128)S(1)} %bitcast.30) | data formatting | bytes 2097152 | tf_op jit(solution)/shard_map/reshape | solution.py:568
  90.6 1.8 %copy.44 = f32[2,64,2048]{2,0,1:T(2,128)} copy(f32[2,64,2048]{2,1,0:T(8,128)S(1)} %bitcast.29) | data formatting | bytes 2097152 | tf_op jit(solution)/shard_map/reshape | solution.py:568
  (25 shorter events, 0.2 us)
Async XLA Ops:
  1.6 2.9 %copy-start.7 = (f32[64,2,2048]{2,1,0:T(2,128)S(1)}, f32[64,2,2048]{2,1,0:T(2,128)}, u32[]{:S(2)}) copy-start(f32[64,2,2048]{2,1,0:T(2,128)} %param.7) | copy-start | bytes 3145732
  4.4 0.8 copy-start.6
  5.1 3.5 %copy-start.8 = (s32[2048]{0:T(1024)S(1)}, s32[2048]{0:T(1024)}, u32[]{:S(2)}) copy-start(s32[2048]{0:T(1024)} %param.13) | copy-start | bytes 24580
  5.1 4.0 %copy-start.9 = (s32[4,2,1024]{2,1,0:T(2,128)S(1)}, s32[4,2,1024]{2,1,0:T(2,128)}, u32[]{:S(2)}) copy-start(s32[4,2,1024]{2,1,0:T(2,128)} %param.9) | copy-start | bytes 98308
  5.1 4.0 %copy-start.11 = (f32[4,4]{1,0:T(4,128)S(1)}, f32[4,4]{1,0:T(4,128)}, u32[]{:S(2)}) copy-start(f32[4,4]{1,0:T(4,128)} %param.10) | copy-start | bytes 196
  5.1 4.7 %copy-start.10 = (f32[4,2,1024]{2,1,0:T(2,128)S(1)}, f32[4,2,1024]{2,1,0:T(2,128)}, u32[]{:S(2)}) copy-start(f32[4,2,1024]{2,1,0:T(2,128)} %param.8) | copy-start | bytes 98308
  7.6 1.0 %copy-start.2 = (f32[2,64,2048]{2,1,0:T(8,128)}, f32[2,64,2048]{2,1,0:T(8,128)S(1)}, u32[]{:S(2)}) copy-start(f32[2,64,2048]{2,1,0:T(8,128)S(1)} %copy.30) | copy-start | bytes 3145732
  10.5 5.6 %copy-start.13 = (f32[8]{0:T(128)S(1)}, f32[8]{0:T(128)}, u32[]{:S(2)}) copy-start(f32[8]{0:T(128)} %constant.29.clone.1) | copy-start | bytes 100
  16.1 24.3 %copy-start = (bf16[4096,512]{1,0:T(8,128)(2,1)}, bf16[4096,512]{1,0:T(8,128)(2,1)S(1)}, u32[]{:S(2)}) copy-start(bf16[4096,512]{1,0:T(8,128)(2,1)S(1)} %table_stage.1.table_ref) | copy-start | bytes 12582916
  37.9 2.5 %copy-start.12 = (f32[8]{0:T(128)S(1)}, f32[8]{0:T(128)}, u32[]{:S(2)}) copy-start(f32[8]{0:T(128)} %constant.28.clone.1) | copy-start | bytes 100
  62.3 1.0 %copy-start.4 = (f32[128,2048]{1,0:T(8,128)}, f32[128,2048]{1,0:T(8,128)S(1)}, u32[]{:S(2)}) copy-start(f32[128,2048]{1,0:T(8,128)S(1)} %multiply_subtract_fusion.1.values_ref) | copy-start | bytes 3145732
  64.0 2.2 %copy-start.1 = (bf16[4096,512]{1,0:T(8,128)(2,1)S(1)}, bf16[4096,512]{1,0:T(8,128)(2,1)}, u32[]{:S(2)}) copy-start(bf16[4096,512]{1,0:T(8,128)(2,1)} %copy-done) | copy-start | bytes 12582916
  82.7 5.6 %copy-start.3 = (f32[2,64,2048]{2,1,0:T(8,128)S(1)}, f32[2,64,2048]{2,1,0:T(8,128)}, u32[]{:S(2)}) copy-start(f32[2,64,2048]{2,1,0:T(8,128)} %copy-done.2) | copy-start | bytes 3145732
  82.7 5.6 %copy-start.5 = (f32[128,2048]{1,0:T(8,128)S(1)}, f32[128,2048]{1,0:T(8,128)}, u32[]{:S(2)}) copy-start(f32[128,2048]{1,0:T(8,128)} %copy-done.4) | copy-start | bytes 3145732

commit v4 on v3

--- a/solution.py
+++ b/solution.py
@@ -112,11 +112,11 @@
     image_ref,
     sums_ref,
     arrived_ref,
-    left_ref,
     shares_ref,
     landed_ref,
     send_sem,
     recv_sem,
+    arrive_sem,
 ):
     total = blk_count * quarter_count
     blk = lax.axis_index("blk")
@@ -132,24 +132,33 @@
     peers(blk_count, quarter_count, greet)
     arrived_ref[me] = send_ref[blk]
     pl.semaphore_wait(barrier, total - 1)
-    scatter(me, blk_count, quarter_count, send_ref, arrived_ref, send_sem.at[0], recv_sem.at[0])
-    some = arrived_ref.at[pl.ds(0, total - 1)]
-    pltpu.make_async_copy(some, some, recv_sem.at[0]).wait()
-
-    arrived = arrived_ref[...].astype(jnp.float32)
-    rows = arrived.shape[1] // 2
-    lanes = arrived.shape[2]
+    scatter(
+        me, blk_count, quarter_count, send_ref, arrived_ref, send_sem.at[0], arrive_sem.at[blk]
+    )
+    rows, lanes = arrived_ref.shape[1] // 2, arrived_ref.shape[2]
+    width = quarter_count * lanes
     lane = lax.broadcasted_iota(jnp.int32, (1, 1, lanes), 2)
     sign = jnp.where(lane < lanes // 2, jnp.float32(1.0), jnp.float32(-1.0))
-    values = arrived[:, :rows]
-    turned = values * cos_ref[...] + pltpu.roll(values, lanes // 2, 2) * sin_ref[...]
-    left = jnp.concatenate([turned, turned * sign], 1).astype(jnp.bfloat16)
-    for d in range(total):
-        left_ref[:, d * lanes : (d + 1) * lanes] = left[d]
-    tail = jnp.sum(arrived[:, rows:], 0)
+    field = jnp.zeros(image_ref.shape, jnp.float32)
+    tail = jnp.zeros((rows, lanes), jnp.float32)
+    for i in range(blk_count):
+        source = lax.rem(blk + blk_count - i, blk_count)
+        base = source * quarter_count
+        some = arrived_ref.at[pl.ds(base, quarter_count - 1 if i == 0 else quarter_count)]
+        pltpu.make_async_copy(some, some, arrive_sem.at[source]).wait()
+        near = pl.ds(base, quarter_count)
+        arrived = arrived_ref[near].astype(jnp.float32)
+        values = arrived[:, :rows]
+        turned = values * cos_ref[near] + pltpu.roll(values, lanes // 2, 2) * sin_ref[near]
+        left = jnp.concatenate([turned, turned * sign], 1).astype(jnp.bfloat16)
+        field += jnp.dot(
+            jnp.concatenate([left[q] for q in range(quarter_count)], 1),
+            table_ref[pl.ds(pl.multiple_of(source * width, width), width), :],
+            preferred_element_type=jnp.float32,
+        )
+        tail += jnp.sum(arrived[:, rows:], 0)
     energy = jnp.sum(jnp.sum(tail, 1, keepdims=True), 0, keepdims=True)
-
-    field = scale * jnp.dot(left_ref[...], table_ref[...], preferred_element_type=jnp.float32)
+    field = scale * field
     params = params_ref[...]
     ratio = params[1:2, 0:1] + params[2:3, 0:1] * energy / params[3:4, 0:1]
     image = params[0:1, 0:1] * field + ratio * old_ref[...]
@@ -220,11 +229,11 @@
         out_specs=(pl.BlockSpec(memory_space=pltpu.VMEM),) * 3,
         scratch_shapes=[
             pltpu.VMEM(block, jnp.bfloat16),
-            pltpu.VMEM((block_rows, total * lanes), jnp.bfloat16),
             pltpu.VMEM(block, jnp.bfloat16),
             pltpu.VMEM(block, jnp.bfloat16),
             pltpu.SemaphoreType.DMA((2,)),
             pltpu.SemaphoreType.DMA((2,)),
+            pltpu.SemaphoreType.DMA((blk_count,)),
         ],
         compiler_params=pltpu.CompilerParams(
             collective_id=2, has_side_effects=True, vmem_limit_bytes=14 << 20
@@ -376,7 +385,7 @@
             )
         return carry
 
-    lax.fori_loop(0, total, fill, 0, unroll=2)
+    lax.fori_loop(0, total, fill, 0, unroll=4)
 
 
 def table_stage(orders, total, half_lon):

time: 92.7 us -> 93.5 us (level)
    pallas_call x1, Pallas kernels: 5.59 us -> 6.75 us  [table_stage(): pl.pallas_call(functools.partial(table_kernel, total), out_shape=jax.Shap...]
where the time goes in v4:
time: 93.5 us; the launch traced here: 93.2 us
  Pallas kernels  71.8 us (77%)
  local copies, waits for them, and re-layouts  14.7 us (16%)
  between operations  4.85 us (5%)
  other arithmetic  1.86 us (2%)
    pallas_call x3, Pallas kernels, grid_stage(): pl.pallas_call(functools.partial(grid_kernel, blk_count, quarter_count, s...  50.4 us
    pallas_call x3, Pallas kernels, synth_stage(): pl.pallas_call(functools.partial(synth_kernel, blk_count), out_shape=jax....  7.31 us
    pallas_call x3, Pallas kernels, adjoint_stage(): pl.pallas_call(functools.partial(adjoint_kernel, blk_count), out_shape=ja...  7.31 us
    pallas_call x1, Pallas kernels, table_stage(): pl.pallas_call(functools.partial(table_kernel, total), out_shape=jax.Shap...  6.75 us
    unnamed x28, local copies, waits for them, and re-layouts  4.24 us
    reshape x2, local copies, waits for them, and re-layouts, body(): out.reshape(2, slot_count, degree_count).transpose(1, 0, 2)  3.56 us
    transpose x1, local copies, waits for them, and re-layouts, body(): legendre.transpose(1, 0, 2).reshape(cycle_pairs * slot_count, degree_count)  2.83 us

profile of v4, /device:TPU:0, one launch (start us, length us, event | category | flops | bytes accessed | tf_op | source)
XLA Modules:
  0.0 93.2 jit_solution(6481051896776860210)
XLA Ops:
  0.6 0.8 fusion.8
  1.4 0.1 maximum_bitcast_fusion
  1.5 0.1 copy.32.sign_ref
  1.6 2.8 %copy.31 = bf16[8,64,2048]{2,1,0:T(8,128)(2,1)S(1)} copy(bf16[8,64,2048]{2,0,1:T(8,128)(2,1)} %bitcast.31) | data formatting | bytes 4194304 | tf_op jit(solution)/shard_map/transpose | solution.py:544
  4.4 0.0 copy-start.6
  4.5 0.6 copy.30
  5.1 0.0 copy-start.8
  5.1 0.0 copy-start.9
  5.1 0.0 copy-start.11
  5.1 0.0 copy-start.10
  5.1 0.1 copy-done.6
  5.2 2.4 %synth_stage.3.send_ref = bf16[8,16,128]{2,1,0:T(8,128)(2,1)S(1)} custom-call(f32[128,2048]{1,0:T(8,128)S(1)} %bitcast.28, f32[1,2048]{1,0:T(1,128)S(1)} %broadcast_in_dim.46.factor_ref, f32[4,2048]{1,0:T(4,128)S(1)} %copy-done.6, f32[128,1]{1,0:T(8,128)S(1)} %copy.32.sign_ref, bf16[512,2048]{1,0:T(8,128)(2,1)S(1)} %bitcast.22), custom_call_target="tpu_custom_call" | custom-call | tf_op jit(solution)/shard_map/synth_stage/pallas_call | solution.py:285
  7.6 0.0 copy-start.2
  7.6 1.0 %copy-done.2 = f32[2,64,2048]{2,1,0:T(8,128)} copy-done((f32[2,64,2048]{2,1,0:T(8,128)}, f32[2,64,2048]{2,1,0:T(8,128)S(1)}, u32[]{:S(2)}) %copy-start.2) | copy-done | bytes 1048600
  8.6 0.1 reshape.78
  8.7 0.1 reshape.77
  8.8 0.1 pad_maximum_fusion.2
  9.1 0.2 select_reduce_fusion
  9.3 0.5 rev.8
  9.8 0.3 rev.7
  10.1 0.4 copy.33.order_ref
  10.5 0.0 copy-start.13
  10.5 6.7 %table_stage.1.table_ref = bf16[4096,512]{1,0:T(8,128)(2,1)S(1)} custom-call(s32[2048,1]{1,0:T(8,128)S(1)} %copy.33.order_ref), custom_call_target="tpu_custom_call" | custom-call | tf_op jit(solution)/shard_map/table_stage/pallas_call | solution.py:392
  17.3 0.1 broadcast_in_dim.45.params_ref
  17.4 19.5 %grid_stage.3 = (f32[8,8,128]{2,1,0:T(8,128)S(1)}, f32[16,512]{1,0:T(8,128)}, f32[8,128]{1,0:T(8,128)}) custom-call(f32[8,128]{1,0:T(8,128)S(1)} %broadcast_in_dim.45.params_ref, bf16[8,16,128]{2,1,0:T(8,128)(2,1)S(1)} %synth_stage.3.send_ref, f32[16,512]{1,0:T(8,128)S(1)} %get-tuple-element.26.old_ref, f32[16,512]{1,0:T(8,128)S(1)} %get-tuple-element.27.weight_ref, ...), custom_call_target="tpu_custom_call" | custom-call | tf_op jit(solution)/shard_map/grid_stage/pallas_call | solution.py:221
  36.9 2.4 %adjoint_stage.3.values_ref = f32[128,2048]{1,0:T(8,128)S(1)} custom-call(f32[8,8,128]{2,1,0:T(8,128)S(1)} %get-tuple-element.8.returned_ref, f32[4,2048]{1,0:T(4,128)S(1)} %copy-done.6, f32[128,1]{1,0:T(8,128)S(1)} %copy.32.sign_ref, bf16[512,2048]{1,0:T(8,128)(2,1)S(1)} %bitcast.23), custom_call_target="tpu_custom_call" | custom-call | tf_op jit(solution)/shard_map/adjoint_stage/pallas_call | solution.py:344
  39.3 0.0 copy-start.12
  39.4 2.4 %synth_stage.4.send_ref = bf16[8,16,128]{2,1,0:T(8,128)(2,1)S(1)} custom-call(f32[128,2048]{1,0:T(8,128)S(1)} %adjoint_stage.3.values_ref, f32[1,2048]{1,0:T(1,128)S(1)} %add_divide_fusion.1.factor_ref, f32[4,2048]{1,0:T(4,128)S(1)} %copy-done.6, f32[128,1]{1,0:T(8,128)S(1)} %copy.32.sign_ref, bf16[512,2048]{1,0:T(8,128)(2,1)S(1)} %bitcast.24), custom_call_target="tpu_custom_call" | custom-call | tf_op jit(solution)/shard_map/synth_stage/pallas_call | solution.py:285
  41.8 0.0 copy-done.12
  41.8 0.1 broadcast_in_dim.44.params_ref
  41.9 14.4 %grid_stage.4 = (f32[8,8,128]{2,1,0:T(8,128)S(1)}, f32[16,512]{1,0:T(8,128)S(1)}, f32[8,128]{1,0:T(8,128)S(1)}) custom-call(f32[8,128]{1,0:T(8,128)S(1)} %broadcast_in_dim.44.params_ref, bf16[8,16,128]{2,1,0:T(8,128)(2,1)S(1)} %synth_stage.4.send_ref, f32[16,512]{1,0:T(8,128)S(1)} %get-tuple-element.26.old_ref, f32[16,512]{1,0:T(8,128)S(1)} %get-tuple-element.27.weight_ref, ...), custom_call_target="tpu_custom_call" | custom-call | tf_op jit(solution)/shard_map/grid_stage/pallas_call | solution.py:221
  56.3 0.5 fusion.13
  58.1 2.4 %adjoint_stage.4 = f32[128,2048]{1,0:T(8,128)S(1)} custom-call(f32[8,8,128]{2,1,0:T(8,128)S(1)} %get-tuple-element.10.returned_ref, f32[4,2048]{1,0:T(4,128)S(1)} %copy-done.6, f32[128,1]{1,0:T(8,128)S(1)} %copy.32.sign_ref, bf16[512,2048]{1,0:T(8,128)(2,1)S(1)} %bitcast.25), custom_call_target="tpu_custom_call" | custom-call | tf_op jit(solution)/shard_map/adjoint_stage/pallas_call | solution.py:344
  60.5 0.1 multiply_subtract_fusion.1.values_ref
  60.7 2.5 %synth_stage.5.send_ref = bf16[8,16,128]{2,1,0:T(8,128)(2,1)S(1)} custom-call(f32[128,2048]{1,0:T(8,128)S(1)} %multiply_subtract_fusion.1.values_ref, f32[1,2048]{1,0:T(1,128)S(1)} %add_divide_fusion.1.factor_ref, f32[4,2048]{1,0:T(4,128)S(1)} %copy-done.6, f32[128,1]{1,0:T(8,128)S(1)} %copy.32.sign_ref, bf16[512,2048]{1,0:T(8,128)(2,1)S(1)} %bitcast.26), custom_call_target="tpu_custom_call" | custom-call | tf_op jit(solution)/shard_map/synth_stage/pallas_call | solution.py:285
  63.1 0.0 copy-start.4
  63.1 1.0 %copy-done.4 = f32[128,2048]{1,0:T(8,128)} copy-done((f32[128,2048]{1,0:T(8,128)}, f32[128,2048]{1,0:T(8,128)S(1)}, u32[]{:S(2)}) %copy-start.4) | copy-done | bytes 1048600
  64.1 0.6 stack.3
  64.7 0.1 broadcast_in_dim.52.params_ref
  64.8 2.2 %copy-done.1 = bf16[4096,512]{1,0:T(8,128)(2,1)S(1)} copy-done((bf16[4096,512]{1,0:T(8,128)(2,1)S(1)}, bf16[4096,512]{1,0:T(8,128)(2,1)}, u32[]{:S(2)}) %copy-start.1) | copy-done | bytes 4194328
  67.0 16.5 %grid_stage.5 = (f32[8,8,128]{2,1,0:T(8,128)S(1)}, f32[16,512]{1,0:T(8,128)}, f32[8,128]{1,0:T(8,128)S(1)}) custom-call(f32[8,128]{1,0:T(8,128)S(1)} %broadcast_in_dim.52.params_ref, bf16[8,16,128]{2,1,0:T(8,128)(2,1)S(1)} %synth_stage.5.send_ref, f32[16,512]{1,0:T(8,128)S(1)} %get-tuple-element.11.old_ref, f32[16,512]{1,0:T(8,128)S(1)} %get-tuple-element.27.weight_ref, ...), custom_call_target="tpu_custom_call" | custom-call | tf_op jit(solution)/shard_map/grid_stage/pallas_call | solution.py:221
  83.5 0.0 copy-start.3
  83.6 0.0 copy-start.5
  83.6 0.6 fusion.12
  86.7 2.4 %adjoint_stage.5 = f32[128,2048]{1,0:T(8,128)S(1)} custom-call(f32[8,8,128]{2,1,0:T(8,128)S(1)} %get-tuple-element.13.returned_ref, f32[4,2048]{1,0:T(4,128)S(1)} %copy-done.6, f32[128,1]{1,0:T(8,128)S(1)} %copy.32.sign_ref, bf16[512,2048]{1,0:T(8,128)(2,1)S(1)} %bitcast.27), custom_call_target="tpu_custom_call" | custom-call | tf_op jit(solution)/shard_map/adjoint_stage/pallas_call | solution.py:344
  89.2 0.5 multiply_subtract_fusion
  89.7 1.8 %copy.43 = f32[2,64,2048]{2,0,1:T(2,128)} copy(f32[2,64,2048]{2,1,0:T(8,128)S(1)} %bitcast.30) | data formatting | bytes 2097152 | tf_op jit(solution)/shard_map/reshape | solution.py:577
  91.4 1.8 %copy.44 = f32[2,64,2048]{2,0,1:T(2,128)} copy(f32[2,64,2048]{2,1,0:T(8,128)S(1)} %bitcast.29) | data formatting | bytes 2097152 | tf_op jit(solution)/shard_map/reshape | solution.py:577
  (25 shorter events, 0.2 us)
Async XLA Ops:
  1.6 2.9 %copy-start.7 = (f32[64,2,2048]{2,1,0:T(2,128)S(1)}, f32[64,2,2048]{2,1,0:T(2,128)}, u32[]{:S(2)}) copy-start(f32[64,2,2048]{2,1,0:T(2,128)} %param.7) | copy-start | bytes 3145732
  4.4 0.8 copy-start.6
  5.1 3.5 %copy-start.8 = (s32[2048]{0:T(1024)S(1)}, s32[2048]{0:T(1024)}, u32[]{:S(2)}) copy-start(s32[2048]{0:T(1024)} %param.13) | copy-start | bytes 24580
  5.1 4.0 %copy-start.9 = (s32[4,2,1024]{2,1,0:T(2,128)S(1)}, s32[4,2,1024]{2,1,0:T(2,128)}, u32[]{:S(2)}) copy-start(s32[4,2,1024]{2,1,0:T(2,128)} %param.9) | copy-start | bytes 98308
  5.1 4.0 %copy-start.11 = (f32[4,4]{1,0:T(4,128)S(1)}, f32[4,4]{1,0:T(4,128)}, u32[]{:S(2)}) copy-start(f32[4,4]{1,0:T(4,128)} %param.10) | copy-start | bytes 196
  5.1 4.7 %copy-start.10 = (f32[4,2,1024]{2,1,0:T(2,128)S(1)}, f32[4,2,1024]{2,1,0:T(2,128)}, u32[]{:S(2)}) copy-start(f32[4,2,1024]{2,1,0:T(2,128)} %param.8) | copy-start | bytes 98308
  7.6 1.0 %copy-start.2 = (f32[2,64,2048]{2,1,0:T(8,128)}, f32[2,64,2048]{2,1,0:T(8,128)S(1)}, u32[]{:S(2)}) copy-start(f32[2,64,2048]{2,1,0:T(8,128)S(1)} %copy.30) | copy-start | bytes 3145732
  10.5 6.8 %copy-start.13 = (f32[8]{0:T(128)S(1)}, f32[8]{0:T(128)}, u32[]{:S(2)}) copy-start(f32[8]{0:T(128)} %constant.29.clone.1) | copy-start | bytes 100
  17.3 24.6 %copy-start = (bf16[4096,512]{1,0:T(8,128)(2,1)}, bf16[4096,512]{1,0:T(8,128)(2,1)S(1)}, u32[]{:S(2)}) copy-start(bf16[4096,512]{1,0:T(8,128)(2,1)S(1)} %table_stage.1.table_ref) | copy-start | bytes 12582916
  39.3 2.5 %copy-start.12 = (f32[8]{0:T(128)S(1)}, f32[8]{0:T(128)}, u32[]{:S(2)}) copy-start(f32[8]{0:T(128)} %constant.28.clone.1) | copy-start | bytes 100
  63.1 1.0 %copy-start.4 = (f32[128,2048]{1,0:T(8,128)}, f32[128,2048]{1,0:T(8,128)S(1)}, u32[]{:S(2)}) copy-start(f32[128,2048]{1,0:T(8,128)S(1)} %multiply_subtract_fusion.1.values_ref) | copy-start | bytes 3145732
  64.8 2.2 %copy-start.1 = (bf16[4096,512]{1,0:T(8,128)(2,1)S(1)}, bf16[4096,512]{1,0:T(8,128)(2,1)}, u32[]{:S(2)}) copy-start(bf16[4096,512]{1,0:T(8,128)(2,1)} %copy-done) | copy-start | bytes 12582916
  83.5 5.6 %copy-start.3 = (f32[2,64,2048]{2,1,0:T(8,128)S(1)}, f32[2,64,2048]{2,1,0:T(8,128)}, u32[]{:S(2)}) copy-start(f32[2,64,2048]{2,1,0:T(8,128)} %copy-done.2) | copy-start | bytes 3145732
  83.6 5.6 %copy-start.5 = (f32[128,2048]{1,0:T(8,128)S(1)}, f32[128,2048]{1,0:T(8,128)}, u32[]{:S(2)}) copy-start(f32[128,2048]{1,0:T(8,128)} %copy-done.4) | copy-start | bytes 3145732
